TPU v7x, 32 devices: a whole 2x2x4 slice. The times are simulated.
32 devices in a mesh: ctx: 32 (over z, y, x, core), head: 1.
Axes of the slice: x: 2, y: 2, z: 4, core: 2. Of those that a mesh axis runs over, the one named last changes fastest.
Arguments:
- queries: bfloat16 [4096, 4096], P(('ctx', 'head')), may hold values from -5 to 5
- key_states: bfloat16 [4096, 512], P('ctx', 'head'), may hold values from -5 to 5
- value_states: bfloat16 [4096, 512], P('ctx', 'head'), may hold values from -6 to 6
- outputs: bfloat16 [4096, 4096], P(('ctx', 'head')), may hold values from -6 to 6
- out_grad: bfloat16 [4096, 4096], P(('ctx', 'head')), may hold values from -6 to 6
- doc_of_tile: int32 [32], replicated, may hold values from 0 to 3, never falling along the last dimension, each value on 1 to 16 neighbouring positions
- tile_position: int32 [32], replicated, may hold values from 0 to 31, each once
Outputs:
- query_grad: bfloat16 [4096, 4096], P('ctx', 'head')
- key_grad: bfloat16 [4096, 512], P('ctx', 'head')
- value_grad: bfloat16 [4096, 512], P('ctx', 'head')
Inputs may be any that keep to these rules, and one draw needn't show every extreme that they name: `doc_of_tile`: each document is a run of whole tiles in sequence order, 1 to 16 tiles long, one exactly 16. `tile_position`: a permutation of the 32 sequence tiles.
All inputs are finite; a program needn't handle non-finite values.
Results may differ from a plain program's by a relative error of at most 0.005.
Values may be sent and summed in bfloat16 or wider, within the bound.
A program may use at most 64 MiB of HBM per device.

v0:
```python
import jax
import jax.numpy as jnp
from jax import lax
from jax.sharding import PartitionSpec as P

HD = 128
TILE = 128


def passed_along(value, axis, steps):
    count = lax.axis_size(axis)
    pairs = [(source, (source + steps) % count) for source in range(count)]
    return lax.ppermute(value, axis, pairs)


def layout_rows(first_row, count, tile_position, doc_of_tile):
    row_ids = first_row + jnp.arange(count, dtype=jnp.int32)
    tile_ids = row_ids // TILE
    columns = jnp.arange(tile_position.shape[0], dtype=jnp.int32)
    placed = jnp.sum(
        jnp.where(tile_ids[:, None] == columns[None, :], tile_position[None, :], 0), axis=1
    )
    positions = placed * TILE + row_ids % TILE
    documents = jnp.sum(
        jnp.where(placed[:, None] == columns[None, :], doc_of_tile[None, :], 0), axis=1
    )
    return (positions, documents)


def block_terms(
    query_heads,
    grad_heads,
    log_total,
    delta_heads,
    query_pos,
    query_doc,
    key_block,
    value_block,
    key_pos,
    key_doc,
):
    score_scale = HD ** (-0.5)
    visible = (query_doc[:, None] == key_doc[None, :]) & (key_pos[None, :] <= query_pos[:, None])
    key_rows = key_block.shape[0]
    key_width = key_block.shape[1] * HD
    scores = (
        jnp.einsum("qkgd,pkd->kgqp", query_heads, key_block, preferred_element_type=jnp.float32)
        * score_scale
    )
    probs = jnp.exp(jnp.where(visible, scores - log_total[..., None], -1e30))
    probs_low = probs.astype(jnp.bfloat16)
    grad_probs = jnp.einsum(
        "qkgd,pkd->kgqp", grad_heads, value_block, preferred_element_type=jnp.float32
    )
    grad_scores = (probs * (grad_probs - delta_heads[..., None]) * score_scale).astype(jnp.bfloat16)
    results = []
    results.append(
        jnp.einsum("kgqp,pkd->qkgd", grad_scores, key_block, preferred_element_type=jnp.float32)
    )
    key_part = jnp.einsum(
        "kgqp,qkgd->pkd", grad_scores, query_heads, preferred_element_type=jnp.float32
    )
    value_part = jnp.einsum(
        "kgqp,qkgd->pkd", probs_low, grad_heads, preferred_element_type=jnp.float32
    )
    results.append(
        jnp.concatenate(
            [key_part.reshape(key_rows, key_width), value_part.reshape(key_rows, key_width)], axis=1
        )
    )
    return tuple(results)


def local(queries, key_states, value_states, outputs, out_grad, doc_of_tile, tile_position):
    query_local, output_local, grad_local = (
        lax.all_to_all(queries, "head", split_axis=1, concat_axis=0, tiled=True),
        lax.all_to_all(outputs, "head", split_axis=1, concat_axis=0, tiled=True),
        lax.all_to_all(out_grad, "head", split_axis=1, concat_axis=0, tiled=True),
    )
    rows = query_local.shape[0]
    products = grad_local.astype(jnp.float32) * output_local.astype(jnp.float32)
    delta_local = jnp.sum(products.reshape(rows, -1, HD), axis=-1)
    kv_heads = key_states.shape[1] // HD
    groups = query_local.shape[1] // (kv_heads * HD)
    query_heads = query_local.reshape(rows, kv_heads, groups, HD)
    grad_heads = grad_local.reshape(rows, kv_heads, groups, HD)
    delta_heads = jnp.transpose(delta_local.reshape(rows, kv_heads, groups), (1, 2, 0))
    my_index = lax.axis_index("ctx")
    query_pos, query_doc = layout_rows(my_index * rows, rows, tile_position, doc_of_tile)
    score_scale = HD ** (-0.5)
    start_state = (
        jnp.full((kv_heads, groups, rows), -1e30, jnp.float32),
        jnp.zeros((kv_heads, groups, rows), jnp.float32),
    )
    piece = lax.all_gather(key_states, "ctx", axis=0, tiled=True)
    count = piece.shape[0]
    span = min(count, rows)
    pieces = count // span

    def absorb(state, piece_index):
        running_max, running_sum = state
        begin = piece_index * span
        block = lax.dynamic_slice_in_dim(piece, begin, span, 0).reshape(span, kv_heads, HD)
        key_pos, key_doc = layout_rows(begin, span, tile_position, doc_of_tile)
        visible = (query_doc[:, None] == key_doc[None, :]) & (
            key_pos[None, :] <= query_pos[:, None]
        )
        scores = (
            jnp.einsum("qkgd,pkd->kgqp", query_heads, block, preferred_element_type=jnp.float32)
            * score_scale
        )
        block_max = jnp.max(jnp.where(visible, scores, -1e30), axis=-1)
        new_max = jnp.maximum(running_max, block_max)
        added = jnp.sum(jnp.exp(jnp.where(visible, scores - new_max[..., None], -1e30)), axis=-1)
        new_sum = running_sum * jnp.exp(running_max - new_max) + added
        return ((new_max, new_sum), None)

    state, unused = lax.scan(absorb, start_state, jnp.arange(pieces, dtype=jnp.int32))
    final_max, final_sum = state
    log_total = final_max + jnp.log(final_sum)
    key_width = kv_heads * HD
    ctx_count = lax.axis_size("ctx")

    def turn(step_index, carry):
        key_block, value_block, key_grads, query_sum = carry
        source = (my_index - step_index) % ctx_count
        key_pos, key_doc = layout_rows(source * rows, rows, tile_position, doc_of_tile)
        query_term, key_term = block_terms(
            query_heads,
            grad_heads,
            log_total,
            delta_heads,
            query_pos,
            query_doc,
            key_block.reshape(rows, kv_heads, HD),
            value_block.reshape(rows, kv_heads, HD),
            key_pos,
            key_doc,
        )
        key_grads = key_grads + key_term
        query_sum = query_sum + query_term
        key_block, value_block = passed_along((key_block, value_block), "ctx", 1)
        key_grads = passed_along(key_grads, "ctx", 1)
        return (key_block, value_block, key_grads, query_sum)

    start_carry = (
        key_states,
        value_states,
        jnp.zeros((rows, 2 * key_width), jnp.float32),
        jnp.zeros(query_heads.shape, jnp.float32),
    )
    unused_keys, unused_values, key_grads, query_sum = lax.fori_loop(
        0, ctx_count, turn, start_carry
    )
    query_grad = query_sum.reshape(rows, -1).astype(jnp.bfloat16)
    key_grad = key_grads[:, :key_width].astype(jnp.bfloat16)
    value_grad = key_grads[:, key_width:].astype(jnp.bfloat16)
    return (query_grad, key_grad, value_grad)


def solution(mesh):
    placed = (
        P(("ctx", "head"), None),
        P("ctx", "head"),
        P("ctx", "head"),
        P(("ctx", "head"), None),
        P(("ctx", "head"), None),
        P(),
        P(),
    )
    return jax.shard_map(
        local,
        mesh=mesh,
        in_specs=placed,
        out_specs=(P("ctx", "head"), P("ctx", "head"), P("ctx", "head")),
        check_vma=False,
    )
```

profile of v0, /device:TPU:0, one launch (start us, length us, event | category | flops | bytes accessed | tf_op | source)
XLA Modules:
  0.0 1060.9 jit_solution(4308797256564817871)
XLA Ops:
  24.3 55.9 %all-gather.2.cloned.1.call-done = bf16[4096,512]{0,1:T(8,128)(2,1)} async-done(((bf16[128,512]{0,1:T(8,128)(2,1)}), bf16[4096,512]{0,1:T(8,128)(2,1)}) %all-gather.2.cloned.1.call-update) | async-done | bytes 4194320 | tf_op jit(solution)/shard_map/all_gather | solution.py:95
  80.3 176.0 %while.38 = (s32[]{:T(128)}, f32[4,8,128]{2,1,0:T(8,128)S(1)}, f32[4,8,128]{2,1,0:T(8,128)S(1)}, s32[128]{0:T(128)}, s32[32]{0:T(128)S(1)}, /*index=5*/s32[32]{0...) while((s32[]{:T(128)}, f32[4,8,128]{2,1,0:T(8,128)S(1)}, ...), condition=%wide.region_7.8_spmd.clone, body=%wide.region_2.7_spmd.clone.sunk | while | flops 137985536 | bytes 5904350 | solution.py:118
  257.7 790.6 %while.39 = (s32[]{:T(128)}, bf16[128,512]{1,0:T(8,128)(2,1)}, bf16[128,512]{1,0:T(8,128)(2,1)}, f32[128,1024]{0,1:T(8,128)}, f32[128,4,8,128]{3,0,2,1:T(8,128)}...) while((s32[]{:T(128)}, bf16[128,512]{1,0:T(8,128)(2,1)}, ...), condition=%wide.region_12.13_spmd.clone, body=%wide.region_9.12_spmd.clone.sunk | while | flops 676670976 | bytes 25630960 | solution.py:152
  270.6 10.4 collective-permute-done
  291.8 3.5 bitcast_add_fusion.2
  295.3 10.4 collective-permute-done
  316.5 3.5 bitcast_add_fusion.2
  320.0 10.4 collective-permute-done
  341.2 3.5 bitcast_add_fusion.2
  344.7 10.4 collective-permute-done
  366.0 3.5 bitcast_add_fusion.2
  369.4 10.4 collective-permute-done
  390.7 3.5 bitcast_add_fusion.2
  394.1 10.4 collective-permute-done
  415.4 3.5 bitcast_add_fusion.2
  418.8 10.4 collective-permute-done
  440.1 3.5 bitcast_add_fusion.2
  443.6 10.4 collective-permute-done
  464.8 3.5 bitcast_add_fusion.2
  468.3 10.4 collective-permute-done
  489.5 3.5 bitcast_add_fusion.2
  493.0 10.4 collective-permute-done
  514.2 3.5 bitcast_add_fusion.2
  517.7 10.4 collective-permute-done
  538.9 3.5 bitcast_add_fusion.2
  542.4 10.4 collective-permute-done
  563.6 3.5 bitcast_add_fusion.2
  567.1 10.4 collective-permute-done
  588.3 3.5 bitcast_add_fusion.2
  591.8 10.4 collective-permute-done
  613.0 3.5 bitcast_add_fusion.2
  616.5 10.4 collective-permute-done
  637.7 3.5 bitcast_add_fusion.2
  641.2 10.4 collective-permute-done
  662.4 3.5 bitcast_add_fusion.2
  665.9 10.4 collective-permute-done
  687.2 3.5 bitcast_add_fusion.2
  690.6 10.4 collective-permute-done
  711.9 3.5 bitcast_add_fusion.2
  715.3 10.4 collective-permute-done
  736.6 3.5 bitcast_add_fusion.2
  740.0 10.4 collective-permute-done
  761.3 3.5 bitcast_add_fusion.2
  764.7 10.4 collective-permute-done
  786.0 3.5 bitcast_add_fusion.2
  789.4 10.4 collective-permute-done
  810.7 3.5 bitcast_add_fusion.2
  814.2 10.4 collective-permute-done
  835.4 3.5 bitcast_add_fusion.2
  838.9 10.4 collective-permute-done
  860.1 3.5 bitcast_add_fusion.2
  863.6 10.4 collective-permute-done
  884.8 3.5 bitcast_add_fusion.2
  888.3 10.4 collective-permute-done
  909.5 3.5 bitcast_add_fusion.2
  913.0 10.4 collective-permute-done
  934.2 3.5 bitcast_add_fusion.2
  937.7 10.4 collective-permute-done
  958.9 3.5 bitcast_add_fusion.2
  962.4 10.4 collective-permute-done
  983.6 3.5 bitcast_add_fusion.2
  987.1 10.4 collective-permute-done
  1011.8 10.4 collective-permute-done
  1036.5 10.4 collective-permute-done
  (1150 shorter events, 532.8 us)
Async XLA Ops:
  7.2 73.1 %all-gather.2.cloned.1.call-start = ((), (), s32[]{:S(2)}) async-start(), calls=%async_computation | async-start | bytes 4325376 | tf_op jit(solution)/shard_map/all_gather | solution.py:95
  267.0 15.3 %collective-permute-start.2 = (f32[128,1024]{0,1:T(8,128)}, f32[128,1024]{0,1:T(8,128)}, u32[]{:S(2)}, u32[]{:S(2)}) collective-permute-start(f32[128,1024]{0,1:T(8,128)} %maximum_add_fusion.2), channel_id=1, source_target_pairs={{0,1},{1,2},{2,3},{3,4},{4,5},{5,6},{6,7},{7,8},{8,9},{9,10},{10,1... | collective-permute-start | bytes 1572872 | tf_op jit(solution)/shard_map/while/body/eval_jaxpr/ppermute | solution.py:13
  291.7 15.3 %collective-permute-start.2 = (f32[128,1024]{0,1:T(8,128)}, f32[128,1024]{0,1:T(8,128)}, u32[]{:S(2)}, u32[]{:S(2)}) collective-permute-start(f32[128,1024]{0,1:T(8,128)} %maximum_add_fusion.2), channel_id=1, source_target_pairs={{0,1},{1,2},{2,3},{3,4},{4,5},{5,6},{6,7},{7,8},{8,9},{9,10},{10,1... | collective-permute-start | bytes 1572872 | tf_op jit(solution)/shard_map/while/body/eval_jaxpr/ppermute | solution.py:13
  291.8 15.3 %collective-permute-start.1 = (bf16[128,512]{1,0:T(8,128)(2,1)S(1)}, bf16[128,512]{1,0:T(8,128)(2,1)}, u32[]{:S(2)}, u32[]{:S(2)}) collective-permute-start(bf16[128,512]{1,0:T(8,128)(2,1)S(1)} %copy.137), channel_id=1, source_target_pairs={{0,1},{1,2},{2,3},{3,4},{4,5},{5,6},{6,7},{7,8},{8,9},{9,10},{10,1... | collective-permute-start | bytes 393224 | tf_op jit(solution)/shard_map/while/body/eval_jaxpr/ppermute | solution.py:13
  316.5 15.3 %collective-permute-start.2 = (f32[128,1024]{0,1:T(8,128)}, f32[128,1024]{0,1:T(8,128)}, u32[]{:S(2)}, u32[]{:S(2)}) collective-permute-start(f32[128,1024]{0,1:T(8,128)} %maximum_add_fusion.2), channel_id=1, source_target_pairs={{0,1},{1,2},{2,3},{3,4},{4,5},{5,6},{6,7},{7,8},{8,9},{9,10},{10,1... | collective-permute-start | bytes 1572872 | tf_op jit(solution)/shard_map/while/body/eval_jaxpr/ppermute | solution.py:13
  316.5 15.3 %collective-permute-start.1 = (bf16[128,512]{1,0:T(8,128)(2,1)S(1)}, bf16[128,512]{1,0:T(8,128)(2,1)}, u32[]{:S(2)}, u32[]{:S(2)}) collective-permute-start(bf16[128,512]{1,0:T(8,128)(2,1)S(1)} %copy.137), channel_id=1, source_target_pairs={{0,1},{1,2},{2,3},{3,4},{4,5},{5,6},{6,7},{7,8},{8,9},{9,10},{10,1... | collective-permute-start | bytes 393224 | tf_op jit(solution)/shard_map/while/body/eval_jaxpr/ppermute | solution.py:13
  341.2 15.3 %collective-permute-start.2 = (f32[128,1024]{0,1:T(8,128)}, f32[128,1024]{0,1:T(8,128)}, u32[]{:S(2)}, u32[]{:S(2)}) collective-permute-start(f32[128,1024]{0,1:T(8,128)} %maximum_add_fusion.2), channel_id=1, source_target_pairs={{0,1},{1,2},{2,3},{3,4},{4,5},{5,6},{6,7},{7,8},{8,9},{9,10},{10,1... | collective-permute-start | bytes 1572872 | tf_op jit(solution)/shard_map/while/body/eval_jaxpr/ppermute | solution.py:13
  341.2 15.3 %collective-permute-start.1 = (bf16[128,512]{1,0:T(8,128)(2,1)S(1)}, bf16[128,512]{1,0:T(8,128)(2,1)}, u32[]{:S(2)}, u32[]{:S(2)}) collective-permute-start(bf16[128,512]{1,0:T(8,128)(2,1)S(1)} %copy.137), channel_id=1, source_target_pairs={{0,1},{1,2},{2,3},{3,4},{4,5},{5,6},{6,7},{7,8},{8,9},{9,10},{10,1... | collective-permute-start | bytes 393224 | tf_op jit(solution)/shard_map/while/body/eval_jaxpr/ppermute | solution.py:13
  365.9 15.3 %collective-permute-start.2 = (f32[128,1024]{0,1:T(8,128)}, f32[128,1024]{0,1:T(8,128)}, u32[]{:S(2)}, u32[]{:S(2)}) collective-permute-start(f32[128,1024]{0,1:T(8,128)} %maximum_add_fusion.2), channel_id=1, source_target_pairs={{0,1},{1,2},{2,3},{3,4},{4,5},{5,6},{6,7},{7,8},{8,9},{9,10},{10,1... | collective-permute-start | bytes 1572872 | tf_op jit(solution)/shard_map/while/body/eval_jaxpr/ppermute | solution.py:13
  365.9 15.3 %collective-permute-start.1 = (bf16[128,512]{1,0:T(8,128)(2,1)S(1)}, bf16[128,512]{1,0:T(8,128)(2,1)}, u32[]{:S(2)}, u32[]{:S(2)}) collective-permute-start(bf16[128,512]{1,0:T(8,128)(2,1)S(1)} %copy.137), channel_id=1, source_target_pairs={{0,1},{1,2},{2,3},{3,4},{4,5},{5,6},{6,7},{7,8},{8,9},{9,10},{10,1... | collective-permute-start | bytes 393224 | tf_op jit(solution)/shard_map/while/body/eval_jaxpr/ppermute | solution.py:13
  390.6 15.3 %collective-permute-start.2 = (f32[128,1024]{0,1:T(8,128)}, f32[128,1024]{0,1:T(8,128)}, u32[]{:S(2)}, u32[]{:S(2)}) collective-permute-start(f32[128,1024]{0,1:T(8,128)} %maximum_add_fusion.2), channel_id=1, source_target_pairs={{0,1},{1,2},{2,3},{3,4},{4,5},{5,6},{6,7},{7,8},{8,9},{9,10},{10,1... | collective-permute-start | bytes 1572872 | tf_op jit(solution)/shard_map/while/body/eval_jaxpr/ppermute | solution.py:13
  390.6 15.3 %collective-permute-start.1 = (bf16[128,512]{1,0:T(8,128)(2,1)S(1)}, bf16[128,512]{1,0:T(8,128)(2,1)}, u32[]{:S(2)}, u32[]{:S(2)}) collective-permute-start(bf16[128,512]{1,0:T(8,128)(2,1)S(1)} %copy.137), channel_id=1, source_target_pairs={{0,1},{1,2},{2,3},{3,4},{4,5},{5,6},{6,7},{7,8},{8,9},{9,10},{10,1... | collective-permute-start | bytes 393224 | tf_op jit(solution)/shard_map/while/body/eval_jaxpr/ppermute | solution.py:13
  415.3 15.3 %collective-permute-start.2 = (f32[128,1024]{0,1:T(8,128)}, f32[128,1024]{0,1:T(8,128)}, u32[]{:S(2)}, u32[]{:S(2)}) collective-permute-start(f32[128,1024]{0,1:T(8,128)} %maximum_add_fusion.2), channel_id=1, source_target_pairs={{0,1},{1,2},{2,3},{3,4},{4,5},{5,6},{6,7},{7,8},{8,9},{9,10},{10,1... | collective-permute-start | bytes 1572872 | tf_op jit(solution)/shard_map/while/body/eval_jaxpr/ppermute | solution.py:13
  415.3 15.3 %collective-permute-start.1 = (bf16[128,512]{1,0:T(8,128)(2,1)S(1)}, bf16[128,512]{1,0:T(8,128)(2,1)}, u32[]{:S(2)}, u32[]{:S(2)}) collective-permute-start(bf16[128,512]{1,0:T(8,128)(2,1)S(1)} %copy.137), channel_id=1, source_target_pairs={{0,1},{1,2},{2,3},{3,4},{4,5},{5,6},{6,7},{7,8},{8,9},{9,10},{10,1... | collective-permute-start | bytes 393224 | tf_op jit(solution)/shard_map/while/body/eval_jaxpr/ppermute | solution.py:13
  440.0 15.3 %collective-permute-start.2 = (f32[128,1024]{0,1:T(8,128)}, f32[128,1024]{0,1:T(8,128)}, u32[]{:S(2)}, u32[]{:S(2)}) collective-permute-start(f32[128,1024]{0,1:T(8,128)} %maximum_add_fusion.2), channel_id=1, source_target_pairs={{0,1},{1,2},{2,3},{3,4},{4,5},{5,6},{6,7},{7,8},{8,9},{9,10},{10,1... | collective-permute-start | bytes 1572872 | tf_op jit(solution)/shard_map/while/body/eval_jaxpr/ppermute | solution.py:13
  440.0 15.3 %collective-permute-start.1 = (bf16[128,512]{1,0:T(8,128)(2,1)S(1)}, bf16[128,512]{1,0:T(8,128)(2,1)}, u32[]{:S(2)}, u32[]{:S(2)}) collective-permute-start(bf16[128,512]{1,0:T(8,128)(2,1)S(1)} %copy.137), channel_id=1, source_target_pairs={{0,1},{1,2},{2,3},{3,4},{4,5},{5,6},{6,7},{7,8},{8,9},{9,10},{10,1... | collective-permute-start | bytes 393224 | tf_op jit(solution)/shard_map/while/body/eval_jaxpr/ppermute | solution.py:13
  464.7 15.3 %collective-permute-start.2 = (f32[128,1024]{0,1:T(8,128)}, f32[128,1024]{0,1:T(8,128)}, u32[]{:S(2)}, u32[]{:S(2)}) collective-permute-start(f32[128,1024]{0,1:T(8,128)} %maximum_add_fusion.2), channel_id=1, source_target_pairs={{0,1},{1,2},{2,3},{3,4},{4,5},{5,6},{6,7},{7,8},{8,9},{9,10},{10,1... | collective-permute-start | bytes 1572872 | tf_op jit(solution)/shard_map/while/body/eval_jaxpr/ppermute | solution.py:13
  464.7 15.3 %collective-permute-start.1 = (bf16[128,512]{1,0:T(8,128)(2,1)S(1)}, bf16[128,512]{1,0:T(8,128)(2,1)}, u32[]{:S(2)}, u32[]{:S(2)}) collective-permute-start(bf16[128,512]{1,0:T(8,128)(2,1)S(1)} %copy.137), channel_id=1, source_target_pairs={{0,1},{1,2},{2,3},{3,4},{4,5},{5,6},{6,7},{7,8},{8,9},{9,10},{10,1... | collective-permute-start | bytes 393224 | tf_op jit(solution)/shard_map/while/body/eval_jaxpr/ppermute | solution.py:13
  489.4 15.3 %collective-permute-start.2 = (f32[128,1024]{0,1:T(8,128)}, f32[128,1024]{0,1:T(8,128)}, u32[]{:S(2)}, u32[]{:S(2)}) collective-permute-start(f32[128,1024]{0,1:T(8,128)} %maximum_add_fusion.2), channel_id=1, source_target_pairs={{0,1},{1,2},{2,3},{3,4},{4,5},{5,6},{6,7},{7,8},{8,9},{9,10},{10,1... | collective-permute-start | bytes 1572872 | tf_op jit(solution)/shard_map/while/body/eval_jaxpr/ppermute | solution.py:13
  489.4 15.3 %collective-permute-start.1 = (bf16[128,512]{1,0:T(8,128)(2,1)S(1)}, bf16[128,512]{1,0:T(8,128)(2,1)}, u32[]{:S(2)}, u32[]{:S(2)}) collective-permute-start(bf16[128,512]{1,0:T(8,128)(2,1)S(1)} %copy.137), channel_id=1, source_target_pairs={{0,1},{1,2},{2,3},{3,4},{4,5},{5,6},{6,7},{7,8},{8,9},{9,10},{10,1... | collective-permute-start | bytes 393224 | tf_op jit(solution)/shard_map/while/body/eval_jaxpr/ppermute | solution.py:13
  514.1 15.3 %collective-permute-start.2 = (f32[128,1024]{0,1:T(8,128)}, f32[128,1024]{0,1:T(8,128)}, u32[]{:S(2)}, u32[]{:S(2)}) collective-permute-start(f32[128,1024]{0,1:T(8,128)} %maximum_add_fusion.2), channel_id=1, source_target_pairs={{0,1},{1,2},{2,3},{3,4},{4,5},{5,6},{6,7},{7,8},{8,9},{9,10},{10,1... | collective-permute-start | bytes 1572872 | tf_op jit(solution)/shard_map/while/body/eval_jaxpr/ppermute | solution.py:13
  514.1 15.3 %collective-permute-start.1 = (bf16[128,512]{1,0:T(8,128)(2,1)S(1)}, bf16[128,512]{1,0:T(8,128)(2,1)}, u32[]{:S(2)}, u32[]{:S(2)}) collective-permute-start(bf16[128,512]{1,0:T(8,128)(2,1)S(1)} %copy.137), channel_id=1, source_target_pairs={{0,1},{1,2},{2,3},{3,4},{4,5},{5,6},{6,7},{7,8},{8,9},{9,10},{10,1... | collective-permute-start | bytes 393224 | tf_op jit(solution)/shard_map/while/body/eval_jaxpr/ppermute | solution.py:13
  538.8 15.3 %collective-permute-start.2 = (f32[128,1024]{0,1:T(8,128)}, f32[128,1024]{0,1:T(8,128)}, u32[]{:S(2)}, u32[]{:S(2)}) collective-permute-start(f32[128,1024]{0,1:T(8,128)} %maximum_add_fusion.2), channel_id=1, source_target_pairs={{0,1},{1,2},{2,3},{3,4},{4,5},{5,6},{6,7},{7,8},{8,9},{9,10},{10,1... | collective-permute-start | bytes 1572872 | tf_op jit(solution)/shard_map/while/body/eval_jaxpr/ppermute | solution.py:13
  538.8 15.3 %collective-permute-start.1 = (bf16[128,512]{1,0:T(8,128)(2,1)S(1)}, bf16[128,512]{1,0:T(8,128)(2,1)}, u32[]{:S(2)}, u32[]{:S(2)}) collective-permute-start(bf16[128,512]{1,0:T(8,128)(2,1)S(1)} %copy.137), channel_id=1, source_target_pairs={{0,1},{1,2},{2,3},{3,4},{4,5},{5,6},{6,7},{7,8},{8,9},{9,10},{10,1... | collective-permute-start | bytes 393224 | tf_op jit(solution)/shard_map/while/body/eval_jaxpr/ppermute | solution.py:13
  563.5 15.3 %collective-permute-start.2 = (f32[128,1024]{0,1:T(8,128)}, f32[128,1024]{0,1:T(8,128)}, u32[]{:S(2)}, u32[]{:S(2)}) collective-permute-start(f32[128,1024]{0,1:T(8,128)} %maximum_add_fusion.2), channel_id=1, source_target_pairs={{0,1},{1,2},{2,3},{3,4},{4,5},{5,6},{6,7},{7,8},{8,9},{9,10},{10,1... | collective-permute-start | bytes 1572872 | tf_op jit(solution)/shard_map/while/body/eval_jaxpr/ppermute | solution.py:13
  563.5 15.3 %collective-permute-start.1 = (bf16[128,512]{1,0:T(8,128)(2,1)S(1)}, bf16[128,512]{1,0:T(8,128)(2,1)}, u32[]{:S(2)}, u32[]{:S(2)}) collective-permute-start(bf16[128,512]{1,0:T(8,128)(2,1)S(1)} %copy.137), channel_id=1, source_target_pairs={{0,1},{1,2},{2,3},{3,4},{4,5},{5,6},{6,7},{7,8},{8,9},{9,10},{10,1... | collective-permute-start | bytes 393224 | tf_op jit(solution)/shard_map/while/body/eval_jaxpr/ppermute | solution.py:13
  588.2 15.3 %collective-permute-start.2 = (f32[128,1024]{0,1:T(8,128)}, f32[128,1024]{0,1:T(8,128)}, u32[]{:S(2)}, u32[]{:S(2)}) collective-permute-start(f32[128,1024]{0,1:T(8,128)} %maximum_add_fusion.2), channel_id=1, source_target_pairs={{0,1},{1,2},{2,3},{3,4},{4,5},{5,6},{6,7},{7,8},{8,9},{9,10},{10,1... | collective-permute-start | bytes 1572872 | tf_op jit(solution)/shard_map/while/body/eval_jaxpr/ppermute | solution.py:13
  588.3 15.3 %collective-permute-start.1 = (bf16[128,512]{1,0:T(8,128)(2,1)S(1)}, bf16[128,512]{1,0:T(8,128)(2,1)}, u32[]{:S(2)}, u32[]{:S(2)}) collective-permute-start(bf16[128,512]{1,0:T(8,128)(2,1)S(1)} %copy.137), channel_id=1, source_target_pairs={{0,1},{1,2},{2,3},{3,4},{4,5},{5,6},{6,7},{7,8},{8,9},{9,10},{10,1... | collective-permute-start | bytes 393224 | tf_op jit(solution)/shard_map/while/body/eval_jaxpr/ppermute | solution.py:13
  612.9 15.3 %collective-permute-start.2 = (f32[128,1024]{0,1:T(8,128)}, f32[128,1024]{0,1:T(8,128)}, u32[]{:S(2)}, u32[]{:S(2)}) collective-permute-start(f32[128,1024]{0,1:T(8,128)} %maximum_add_fusion.2), channel_id=1, source_target_pairs={{0,1},{1,2},{2,3},{3,4},{4,5},{5,6},{6,7},{7,8},{8,9},{9,10},{10,1... | collective-permute-start | bytes 1572872 | tf_op jit(solution)/shard_map/while/body/eval_jaxpr/ppermute | solution.py:13
  613.0 15.3 %collective-permute-start.1 = (bf16[128,512]{1,0:T(8,128)(2,1)S(1)}, bf16[128,512]{1,0:T(8,128)(2,1)}, u32[]{:S(2)}, u32[]{:S(2)}) collective-permute-start(bf16[128,512]{1,0:T(8,128)(2,1)S(1)} %copy.137), channel_id=1, source_target_pairs={{0,1},{1,2},{2,3},{3,4},{4,5},{5,6},{6,7},{7,8},{8,9},{9,10},{10,1... | collective-permute-start | bytes 393224 | tf_op jit(solution)/shard_map/while/body/eval_jaxpr/ppermute | solution.py:13
  637.6 15.3 %collective-permute-start.2 = (f32[128,1024]{0,1:T(8,128)}, f32[128,1024]{0,1:T(8,128)}, u32[]{:S(2)}, u32[]{:S(2)}) collective-permute-start(f32[128,1024]{0,1:T(8,128)} %maximum_add_fusion.2), channel_id=1, source_target_pairs={{0,1},{1,2},{2,3},{3,4},{4,5},{5,6},{6,7},{7,8},{8,9},{9,10},{10,1... | collective-permute-start | bytes 1572872 | tf_op jit(solution)/shard_map/while/body/eval_jaxpr/ppermute | solution.py:13
  637.7 15.3 %collective-permute-start.1 = (bf16[128,512]{1,0:T(8,128)(2,1)S(1)}, bf16[128,512]{1,0:T(8,128)(2,1)}, u32[]{:S(2)}, u32[]{:S(2)}) collective-permute-start(bf16[128,512]{1,0:T(8,128)(2,1)S(1)} %copy.137), channel_id=1, source_target_pairs={{0,1},{1,2},{2,3},{3,4},{4,5},{5,6},{6,7},{7,8},{8,9},{9,10},{10,1... | collective-permute-start | bytes 393224 | tf_op jit(solution)/shard_map/while/body/eval_jaxpr/ppermute | solution.py:13
  662.4 15.3 %collective-permute-start.2 = (f32[128,1024]{0,1:T(8,128)}, f32[128,1024]{0,1:T(8,128)}, u32[]{:S(2)}, u32[]{:S(2)}) collective-permute-start(f32[128,1024]{0,1:T(8,128)} %maximum_add_fusion.2), channel_id=1, source_target_pairs={{0,1},{1,2},{2,3},{3,4},{4,5},{5,6},{6,7},{7,8},{8,9},{9,10},{10,1... | collective-permute-start | bytes 1572872 | tf_op jit(solution)/shard_map/while/body/eval_jaxpr/ppermute | solution.py:13
  662.4 15.3 %collective-permute-start.1 = (bf16[128,512]{1,0:T(8,128)(2,1)S(1)}, bf16[128,512]{1,0:T(8,128)(2,1)}, u32[]{:S(2)}, u32[]{:S(2)}) collective-permute-start(bf16[128,512]{1,0:T(8,128)(2,1)S(1)} %copy.137), channel_id=1, source_target_pairs={{0,1},{1,2},{2,3},{3,4},{4,5},{5,6},{6,7},{7,8},{8,9},{9,10},{10,1... | collective-permute-start | bytes 393224 | tf_op jit(solution)/shard_map/while/body/eval_jaxpr/ppermute | solution.py:13
  687.1 15.3 %collective-permute-start.2 = (f32[128,1024]{0,1:T(8,128)}, f32[128,1024]{0,1:T(8,128)}, u32[]{:S(2)}, u32[]{:S(2)}) collective-permute-start(f32[128,1024]{0,1:T(8,128)} %maximum_add_fusion.2), channel_id=1, source_target_pairs={{0,1},{1,2},{2,3},{3,4},{4,5},{5,6},{6,7},{7,8},{8,9},{9,10},{10,1... | collective-permute-start | bytes 1572872 | tf_op jit(solution)/shard_map/while/body/eval_jaxpr/ppermute | solution.py:13
  687.1 15.3 %collective-permute-start.1 = (bf16[128,512]{1,0:T(8,128)(2,1)S(1)}, bf16[128,512]{1,0:T(8,128)(2,1)}, u32[]{:S(2)}, u32[]{:S(2)}) collective-permute-start(bf16[128,512]{1,0:T(8,128)(2,1)S(1)} %copy.137), channel_id=1, source_target_pairs={{0,1},{1,2},{2,3},{3,4},{4,5},{5,6},{6,7},{7,8},{8,9},{9,10},{10,1... | collective-permute-start | bytes 393224 | tf_op jit(solution)/shard_map/while/body/eval_jaxpr/ppermute | solution.py:13
  711.8 15.3 %collective-permute-start.2 = (f32[128,1024]{0,1:T(8,128)}, f32[128,1024]{0,1:T(8,128)}, u32[]{:S(2)}, u32[]{:S(2)}) collective-permute-start(f32[128,1024]{0,1:T(8,128)} %maximum_add_fusion.2), channel_id=1, source_target_pairs={{0,1},{1,2},{2,3},{3,4},{4,5},{5,6},{6,7},{7,8},{8,9},{9,10},{10,1... | collective-permute-start | bytes 1572872 | tf_op jit(solution)/shard_map/while/body/eval_jaxpr/ppermute | solution.py:13
  711.8 15.3 %collective-permute-start.1 = (bf16[128,512]{1,0:T(8,128)(2,1)S(1)}, bf16[128,512]{1,0:T(8,128)(2,1)}, u32[]{:S(2)}, u32[]{:S(2)}) collective-permute-start(bf16[128,512]{1,0:T(8,128)(2,1)S(1)} %copy.137), channel_id=1, source_target_pairs={{0,1},{1,2},{2,3},{3,4},{4,5},{5,6},{6,7},{7,8},{8,9},{9,10},{10,1... | collective-permute-start | bytes 393224 | tf_op jit(solution)/shard_map/while/body/eval_jaxpr/ppermute | solution.py:13
  736.5 15.3 %collective-permute-start.2 = (f32[128,1024]{0,1:T(8,128)}, f32[128,1024]{0,1:T(8,128)}, u32[]{:S(2)}, u32[]{:S(2)}) collective-permute-start(f32[128,1024]{0,1:T(8,128)} %maximum_add_fusion.2), channel_id=1, source_target_pairs={{0,1},{1,2},{2,3},{3,4},{4,5},{5,6},{6,7},{7,8},{8,9},{9,10},{10,1... | collective-permute-start | bytes 1572872 | tf_op jit(solution)/shard_map/while/body/eval_jaxpr/ppermute | solution.py:13
  736.5 15.3 %collective-permute-start.1 = (bf16[128,512]{1,0:T(8,128)(2,1)S(1)}, bf16[128,512]{1,0:T(8,128)(2,1)}, u32[]{:S(2)}, u32[]{:S(2)}) collective-permute-start(bf16[128,512]{1,0:T(8,128)(2,1)S(1)} %copy.137), channel_id=1, source_target_pairs={{0,1},{1,2},{2,3},{3,4},{4,5},{5,6},{6,7},{7,8},{8,9},{9,10},{10,1... | collective-permute-start | bytes 393224 | tf_op jit(solution)/shard_map/while/body/eval_jaxpr/ppermute | solution.py:13
  761.2 15.3 %collective-permute-start.2 = (f32[128,1024]{0,1:T(8,128)}, f32[128,1024]{0,1:T(8,128)}, u32[]{:S(2)}, u32[]{:S(2)}) collective-permute-start(f32[128,1024]{0,1:T(8,128)} %maximum_add_fusion.2), channel_id=1, source_target_pairs={{0,1},{1,2},{2,3},{3,4},{4,5},{5,6},{6,7},{7,8},{8,9},{9,10},{10,1... | collective-permute-start | bytes 1572872 | tf_op jit(solution)/shard_map/while/body/eval_jaxpr/ppermute | solution.py:13
  761.2 15.3 %collective-permute-start.1 = (bf16[128,512]{1,0:T(8,128)(2,1)S(1)}, bf16[128,512]{1,0:T(8,128)(2,1)}, u32[]{:S(2)}, u32[]{:S(2)}) collective-permute-start(bf16[128,512]{1,0:T(8,128)(2,1)S(1)} %copy.137), channel_id=1, source_target_pairs={{0,1},{1,2},{2,3},{3,4},{4,5},{5,6},{6,7},{7,8},{8,9},{9,10},{10,1... | collective-permute-start | bytes 393224 | tf_op jit(solution)/shard_map/while/body/eval_jaxpr/ppermute | solution.py:13
  785.9 15.3 %collective-permute-start.2 = (f32[128,1024]{0,1:T(8,128)}, f32[128,1024]{0,1:T(8,128)}, u32[]{:S(2)}, u32[]{:S(2)}) collective-permute-start(f32[128,1024]{0,1:T(8,128)} %maximum_add_fusion.2), channel_id=1, source_target_pairs={{0,1},{1,2},{2,3},{3,4},{4,5},{5,6},{6,7},{7,8},{8,9},{9,10},{10,1... | collective-permute-start | bytes 1572872 | tf_op jit(solution)/shard_map/while/body/eval_jaxpr/ppermute | solution.py:13
  785.9 15.3 %collective-permute-start.1 = (bf16[128,512]{1,0:T(8,128)(2,1)S(1)}, bf16[128,512]{1,0:T(8,128)(2,1)}, u32[]{:S(2)}, u32[]{:S(2)}) collective-permute-start(bf16[128,512]{1,0:T(8,128)(2,1)S(1)} %copy.137), channel_id=1, source_target_pairs={{0,1},{1,2},{2,3},{3,4},{4,5},{5,6},{6,7},{7,8},{8,9},{9,10},{10,1... | collective-permute-start | bytes 393224 | tf_op jit(solution)/shard_map/while/body/eval_jaxpr/ppermute | solution.py:13
  810.6 15.3 %collective-permute-start.2 = (f32[128,1024]{0,1:T(8,128)}, f32[128,1024]{0,1:T(8,128)}, u32[]{:S(2)}, u32[]{:S(2)}) collective-permute-start(f32[128,1024]{0,1:T(8,128)} %maximum_add_fusion.2), channel_id=1, source_target_pairs={{0,1},{1,2},{2,3},{3,4},{4,5},{5,6},{6,7},{7,8},{8,9},{9,10},{10,1... | collective-permute-start | bytes 1572872 | tf_op jit(solution)/shard_map/while/body/eval_jaxpr/ppermute | solution.py:13
  810.6 15.3 %collective-permute-start.1 = (bf16[128,512]{1,0:T(8,128)(2,1)S(1)}, bf16[128,512]{1,0:T(8,128)(2,1)}, u32[]{:S(2)}, u32[]{:S(2)}) collective-permute-start(bf16[128,512]{1,0:T(8,128)(2,1)S(1)} %copy.137), channel_id=1, source_target_pairs={{0,1},{1,2},{2,3},{3,4},{4,5},{5,6},{6,7},{7,8},{8,9},{9,10},{10,1... | collective-permute-start | bytes 393224 | tf_op jit(solution)/shard_map/while/body/eval_jaxpr/ppermute | solution.py:13
  835.3 15.3 %collective-permute-start.2 = (f32[128,1024]{0,1:T(8,128)}, f32[128,1024]{0,1:T(8,128)}, u32[]{:S(2)}, u32[]{:S(2)}) collective-permute-start(f32[128,1024]{0,1:T(8,128)} %maximum_add_fusion.2), channel_id=1, source_target_pairs={{0,1},{1,2},{2,3},{3,4},{4,5},{5,6},{6,7},{7,8},{8,9},{9,10},{10,1... | collective-permute-start | bytes 1572872 | tf_op jit(solution)/shard_map/while/body/eval_jaxpr/ppermute | solution.py:13
  835.3 15.3 %collective-permute-start.1 = (bf16[128,512]{1,0:T(8,128)(2,1)S(1)}, bf16[128,512]{1,0:T(8,128)(2,1)}, u32[]{:S(2)}, u32[]{:S(2)}) collective-permute-start(bf16[128,512]{1,0:T(8,128)(2,1)S(1)} %copy.137), channel_id=1, source_target_pairs={{0,1},{1,2},{2,3},{3,4},{4,5},{5,6},{6,7},{7,8},{8,9},{9,10},{10,1... | collective-permute-start | bytes 393224 | tf_op jit(solution)/shard_map/while/body/eval_jaxpr/ppermute | solution.py:13
  860.0 15.3 %collective-permute-start.2 = (f32[128,1024]{0,1:T(8,128)}, f32[128,1024]{0,1:T(8,128)}, u32[]{:S(2)}, u32[]{:S(2)}) collective-permute-start(f32[128,1024]{0,1:T(8,128)} %maximum_add_fusion.2), channel_id=1, source_target_pairs={{0,1},{1,2},{2,3},{3,4},{4,5},{5,6},{6,7},{7,8},{8,9},{9,10},{10,1... | collective-permute-start | bytes 1572872 | tf_op jit(solution)/shard_map/while/body/eval_jaxpr/ppermute | solution.py:13
  860.0 15.3 %collective-permute-start.1 = (bf16[128,512]{1,0:T(8,128)(2,1)S(1)}, bf16[128,512]{1,0:T(8,128)(2,1)}, u32[]{:S(2)}, u32[]{:S(2)}) collective-permute-start(bf16[128,512]{1,0:T(8,128)(2,1)S(1)} %copy.137), channel_id=1, source_target_pairs={{0,1},{1,2},{2,3},{3,4},{4,5},{5,6},{6,7},{7,8},{8,9},{9,10},{10,1... | collective-permute-start | bytes 393224 | tf_op jit(solution)/shard_map/while/body/eval_jaxpr/ppermute | solution.py:13
  884.7 15.3 %collective-permute-start.2 = (f32[128,1024]{0,1:T(8,128)}, f32[128,1024]{0,1:T(8,128)}, u32[]{:S(2)}, u32[]{:S(2)}) collective-permute-start(f32[128,1024]{0,1:T(8,128)} %maximum_add_fusion.2), channel_id=1, source_target_pairs={{0,1},{1,2},{2,3},{3,4},{4,5},{5,6},{6,7},{7,8},{8,9},{9,10},{10,1... | collective-permute-start | bytes 1572872 | tf_op jit(solution)/shard_map/while/body/eval_jaxpr/ppermute | solution.py:13
  884.7 15.3 %collective-permute-start.1 = (bf16[128,512]{1,0:T(8,128)(2,1)S(1)}, bf16[128,512]{1,0:T(8,128)(2,1)}, u32[]{:S(2)}, u32[]{:S(2)}) collective-permute-start(bf16[128,512]{1,0:T(8,128)(2,1)S(1)} %copy.137), channel_id=1, source_target_pairs={{0,1},{1,2},{2,3},{3,4},{4,5},{5,6},{6,7},{7,8},{8,9},{9,10},{10,1... | collective-permute-start | bytes 393224 | tf_op jit(solution)/shard_map/while/body/eval_jaxpr/ppermute | solution.py:13
  909.4 15.3 %collective-permute-start.2 = (f32[128,1024]{0,1:T(8,128)}, f32[128,1024]{0,1:T(8,128)}, u32[]{:S(2)}, u32[]{:S(2)}) collective-permute-start(f32[128,1024]{0,1:T(8,128)} %maximum_add_fusion.2), channel_id=1, source_target_pairs={{0,1},{1,2},{2,3},{3,4},{4,5},{5,6},{6,7},{7,8},{8,9},{9,10},{10,1... | collective-permute-start | bytes 1572872 | tf_op jit(solution)/shard_map/while/body/eval_jaxpr/ppermute | solution.py:13
  909.4 15.3 %collective-permute-start.1 = (bf16[128,512]{1,0:T(8,128)(2,1)S(1)}, bf16[128,512]{1,0:T(8,128)(2,1)}, u32[]{:S(2)}, u32[]{:S(2)}) collective-permute-start(bf16[128,512]{1,0:T(8,128)(2,1)S(1)} %copy.137), channel_id=1, source_target_pairs={{0,1},{1,2},{2,3},{3,4},{4,5},{5,6},{6,7},{7,8},{8,9},{9,10},{10,1... | collective-permute-start | bytes 393224 | tf_op jit(solution)/shard_map/while/body/eval_jaxpr/ppermute | solution.py:13
  934.1 15.3 %collective-permute-start.2 = (f32[128,1024]{0,1:T(8,128)}, f32[128,1024]{0,1:T(8,128)}, u32[]{:S(2)}, u32[]{:S(2)}) collective-permute-start(f32[128,1024]{0,1:T(8,128)} %maximum_add_fusion.2), channel_id=1, source_target_pairs={{0,1},{1,2},{2,3},{3,4},{4,5},{5,6},{6,7},{7,8},{8,9},{9,10},{10,1... | collective-permute-start | bytes 1572872 | tf_op jit(solution)/shard_map/while/body/eval_jaxpr/ppermute | solution.py:13
  934.2 15.3 %collective-permute-start.1 = (bf16[128,512]{1,0:T(8,128)(2,1)S(1)}, bf16[128,512]{1,0:T(8,128)(2,1)}, u32[]{:S(2)}, u32[]{:S(2)}) collective-permute-start(bf16[128,512]{1,0:T(8,128)(2,1)S(1)} %copy.137), channel_id=1, source_target_pairs={{0,1},{1,2},{2,3},{3,4},{4,5},{5,6},{6,7},{7,8},{8,9},{9,10},{10,1... | collective-permute-start | bytes 393224 | tf_op jit(solution)/shard_map/while/body/eval_jaxpr/ppermute | solution.py:13
  958.8 15.3 %collective-permute-start.2 = (f32[128,1024]{0,1:T(8,128)}, f32[128,1024]{0,1:T(8,128)}, u32[]{:S(2)}, u32[]{:S(2)}) collective-permute-start(f32[128,1024]{0,1:T(8,128)} %maximum_add_fusion.2), channel_id=1, source_target_pairs={{0,1},{1,2},{2,3},{3,4},{4,5},{5,6},{6,7},{7,8},{8,9},{9,10},{10,1... | collective-permute-start | bytes 1572872 | tf_op jit(solution)/shard_map/while/body/eval_jaxpr/ppermute | solution.py:13
  958.9 15.3 %collective-permute-start.1 = (bf16[128,512]{1,0:T(8,128)(2,1)S(1)}, bf16[128,512]{1,0:T(8,128)(2,1)}, u32[]{:S(2)}, u32[]{:S(2)}) collective-permute-start(bf16[128,512]{1,0:T(8,128)(2,1)S(1)} %copy.137), channel_id=1, source_target_pairs={{0,1},{1,2},{2,3},{3,4},{4,5},{5,6},{6,7},{7,8},{8,9},{9,10},{10,1... | collective-permute-start | bytes 393224 | tf_op jit(solution)/shard_map/while/body/eval_jaxpr/ppermute | solution.py:13
  983.6 15.3 %collective-permute-start.2 = (f32[128,1024]{0,1:T(8,128)}, f32[128,1024]{0,1:T(8,128)}, u32[]{:S(2)}, u32[]{:S(2)}) collective-permute-start(f32[128,1024]{0,1:T(8,128)} %maximum_add_fusion.2), channel_id=1, source_target_pairs={{0,1},{1,2},{2,3},{3,4},{4,5},{5,6},{6,7},{7,8},{8,9},{9,10},{10,1... | collective-permute-start | bytes 1572872 | tf_op jit(solution)/shard_map/while/body/eval_jaxpr/ppermute | solution.py:13
  983.6 15.3 %collective-permute-start.1 = (bf16[128,512]{1,0:T(8,128)(2,1)S(1)}, bf16[128,512]{1,0:T(8,128)(2,1)}, u32[]{:S(2)}, u32[]{:S(2)}) collective-permute-start(bf16[128,512]{1,0:T(8,128)(2,1)S(1)} %copy.137), channel_id=1, source_target_pairs={{0,1},{1,2},{2,3},{3,4},{4,5},{5,6},{6,7},{7,8},{8,9},{9,10},{10,1... | collective-permute-start | bytes 393224 | tf_op jit(solution)/shard_map/while/body/eval_jaxpr/ppermute | solution.py:13
  1008.3 15.3 %collective-permute-start.2 = (f32[128,1024]{0,1:T(8,128)}, f32[128,1024]{0,1:T(8,128)}, u32[]{:S(2)}, u32[]{:S(2)}) collective-permute-start(f32[128,1024]{0,1:T(8,128)} %maximum_add_fusion.2), channel_id=1, source_target_pairs={{0,1},{1,2},{2,3},{3,4},{4,5},{5,6},{6,7},{7,8},{8,9},{9,10},{10,1... | collective-permute-start | bytes 1572872 | tf_op jit(solution)/shard_map/while/body/eval_jaxpr/ppermute | solution.py:13
  1008.3 15.3 %collective-permute-start.1 = (bf16[128,512]{1,0:T(8,128)(2,1)S(1)}, bf16[128,512]{1,0:T(8,128)(2,1)}, u32[]{:S(2)}, u32[]{:S(2)}) collective-permute-start(bf16[128,512]{1,0:T(8,128)(2,1)S(1)} %copy.137), channel_id=1, source_target_pairs={{0,1},{1,2},{2,3},{3,4},{4,5},{5,6},{6,7},{7,8},{8,9},{9,10},{10,1... | collective-permute-start | bytes 393224 | tf_op jit(solution)/shard_map/while/body/eval_jaxpr/ppermute | solution.py:13
  1033.0 15.3 %collective-permute-start.2 = (f32[128,1024]{0,1:T(8,128)}, f32[128,1024]{0,1:T(8,128)}, u32[]{:S(2)}, u32[]{:S(2)}) collective-permute-start(f32[128,1024]{0,1:T(8,128)} %maximum_add_fusion.2), channel_id=1, source_target_pairs={{0,1},{1,2},{2,3},{3,4},{4,5},{5,6},{6,7},{7,8},{8,9},{9,10},{10,1... | collective-permute-start | bytes 1572872 | tf_op jit(solution)/shard_map/while/body/eval_jaxpr/ppermute | solution.py:13
  1033.0 15.3 %collective-permute-start.1 = (bf16[128,512]{1,0:T(8,128)(2,1)S(1)}, bf16[128,512]{1,0:T(8,128)(2,1)}, u32[]{:S(2)}, u32[]{:S(2)}) collective-permute-start(bf16[128,512]{1,0:T(8,128)(2,1)S(1)} %copy.137), channel_id=1, source_target_pairs={{0,1},{1,2},{2,3},{3,4},{4,5},{5,6},{6,7},{7,8},{8,9},{9,10},{10,1... | collective-permute-start | bytes 393224 | tf_op jit(solution)/shard_map/while/body/eval_jaxpr/ppermute | solution.py:13
  (97 other events, 555.6 us)
Sparse Core Ops, SparseCore 0:
  12.1 68.0 all-gather.1
where the time goes:
time: 1070 us; the launch traced here: 1060 us
  waiting for transfers between devices  433 us (40%)
  other arithmetic  229 us (21%)
  matrix products  210 us (20%)
  local copies, waits for them, and re-layouts  145 us (14%)
  loops' own time  25.8 us (2%)
  between operations  14.1 us (1%)
    ppermute x96, waiting for transfers between devices, passed_along(): return lax.ppermute(value, axis, pairs)  377 us
    dot_general x32, matrix products, block_terms(): jnp.einsum('kgqp,pkd->qkgd', grad_scores, key_block, preferred_element_ty...  109 us
    while x224, local copies, waits for them, and re-layouts  79.1 us
    add x32, other arithmetic, turn(): key_grads = key_grads + key_term  60.9 us
    all_gather x1, waiting for transfers between devices, local(): piece = lax.all_gather(key_states, 'ctx', axis=0, tiled=True)  55.9 us
    reduce_sum x65, other arithmetic, layout_rows(): jnp.sum(jnp.where(placed[:, None] == columns[None, :], doc_of_tile[None,...  48.8 us
    reduce_sum x65, other arithmetic, layout_rows(): jnp.sum(jnp.where(tile_ids[:, None] == columns[None, :], tile_position[No...  48.4 us
    dot_general x32, matrix products, block_terms(): jnp.einsum('qkgd,pkd->kgqp', query_heads, key_block, preferred_element_ty...  41.2 us
  transfers between devices with their start and end apart: 97, of which 65 were waited for; matrix products, arithmetic and copies ran while one was open for 11% of the time, Pallas kernels for 0%

commit v1 on v0

v1 whole, which is shorter than its diff:
```python
import functools

import jax
import jax.numpy as jnp
from jax import lax
from jax.experimental import pallas as pl
from jax.experimental.pallas import tpu as pltpu
from jax.sharding import PartitionSpec as P

HD = 128
TILE = 128
SPAN = 2
LOW = -1e30


def kernel(
    heads,
    tiles,
    place_ref,
    place_start_ref,
    inverse_ref,
    qd_ref,
    delta_ref,
    kv_ref,
    dq_ref,
    dkv_ref,
    q_rows,
    q_cols,
    g_rows,
    g_cols,
    score_buf,
    dq_acc,
):
    width = heads * HD
    scale = HD ** (-0.5)
    keys = SPAN * TILE
    dkv_ref[...] = jnp.zeros_like(dkv_ref)
    row_id = lax.broadcasted_iota(jnp.int32, (keys, width), 0)
    col_id = lax.broadcasted_iota(jnp.int32, (keys, width), 1) & (TILE - 1)
    gap = row_id - col_id

    def spots(last):
        found = []
        for offset in range(SPAN):
            where = jnp.maximum(last - (SPAN - 1) + offset, 0)
            found.append(pl.multiple_of(inverse_ref[where] * TILE, TILE))
        return found

    def block(last, begin):
        return jnp.concatenate(
            [kv_ref[pl.ds(spot, TILE), begin : begin + HD] for spot in spots(last)], axis=0
        )

    @pl.loop(0, tiles)
    def _(tile):
        first_row = pl.multiple_of(tile * TILE, TILE)
        place = place_ref[tile]
        start = place_start_ref[tile]
        chunks = (place - start + SPAN) // SPAN
        for h in range(heads):
            lanes = slice(h * HD, (h + 1) * HD)
            q_block = qd_ref[pl.ds(first_row, TILE), h * HD : (h + 1) * HD]
            g_block = qd_ref[pl.ds(first_row, TILE), width + h * HD : width + (h + 1) * HD]
            q_rows[lanes, :] = q_block
            g_rows[lanes, :] = g_block
            q_cols[:, lanes] = q_block.T
            g_cols[:, lanes] = g_block.T

        def totals(step, state):
            top, total = state
            last = place - SPAN * step
            scores = (
                jnp.dot(block(last, 0), q_cols[...], preferred_element_type=jnp.float32) * scale
            )
            first_key = (last - (SPAN - 1)) * TILE
            visible = (gap <= place * TILE - first_key) & (row_id >= start * TILE - first_key)
            scores = jnp.where(visible, scores, LOW)
            score_buf[step] = scores
            new_top = jnp.maximum(top, jnp.max(scores, axis=0, keepdims=True))
            total = total * jnp.exp(top - new_top) + jnp.sum(
                jnp.exp(scores - new_top), axis=0, keepdims=True
            )
            return new_top, total

        top, total = lax.fori_loop(
            0,
            chunks,
            totals,
            (jnp.full((1, width), LOW, jnp.float32), jnp.zeros((1, width), jnp.float32)),
        )
        log_total = top + jnp.log(total)
        delta = delta_ref[tile]
        dq_acc[...] = jnp.zeros_like(dq_acc)

        @pl.loop(0, chunks)
        def _(step):
            last = place - SPAN * step
            k_block = block(last, 0)
            probs = jnp.exp(score_buf[step] - log_total)
            grad_probs = jnp.dot(
                block(last, HD), g_cols[...], preferred_element_type=jnp.float32
            )
            low = probs.astype(jnp.bfloat16)
            grad_scores = (probs * (grad_probs - delta) * scale).astype(jnp.bfloat16)
            dv = jnp.dot(low, g_rows[...], preferred_element_type=jnp.float32)
            dk = jnp.dot(grad_scores, q_rows[...], preferred_element_type=jnp.float32)
            dq_acc[...] += lax.dot_general(
                k_block,
                grad_scores,
                (((0,), (0,)), ((), ())),
                preferred_element_type=jnp.float32,
            )
            for offset, spot in enumerate(spots(last)):
                rows = slice(offset * TILE, (offset + 1) * TILE)
                dkv_ref[pl.ds(spot, TILE), 0:HD] += dk[rows]
                dkv_ref[pl.ds(spot, TILE), HD : 2 * HD] += dv[rows]

        for h in range(heads):
            lanes = slice(h * HD, (h + 1) * HD)
            dq_ref[pl.ds(first_row, TILE), lanes] = dq_acc[:, lanes].T.astype(jnp.bfloat16)


def attention_backward(places, starts, inverse, qd, delta, kv):
    rows, both = qd.shape
    width = both // 2
    heads = width // HD
    tokens = kv.shape[0]
    tiles = rows // TILE
    steps = tokens // TILE // SPAN
    smem = pl.BlockSpec(memory_space=pltpu.SMEM)
    vmem = pl.BlockSpec(memory_space=pltpu.VMEM)
    return pl.pallas_call(
        functools.partial(kernel, heads, tiles),
        out_shape=(
            jax.ShapeDtypeStruct((rows, width), jnp.bfloat16),
            jax.ShapeDtypeStruct((tokens, 2 * HD), jnp.float32),
        ),
        in_specs=[smem, smem, smem, vmem, vmem, vmem],
        out_specs=(vmem, vmem),
        scratch_shapes=[
            pltpu.VMEM((width, HD), jnp.bfloat16),
            pltpu.VMEM((HD, width), jnp.bfloat16),
            pltpu.VMEM((width, HD), jnp.bfloat16),
            pltpu.VMEM((HD, width), jnp.bfloat16),
            pltpu.VMEM((steps // 2 + 1, SPAN * TILE, width), jnp.float32),
            pltpu.VMEM((HD, width), jnp.float32),
        ],
        compiler_params=pltpu.CompilerParams(vmem_limit_bytes=48 * 1024 * 1024),
        cost_estimate=pl.CostEstimate(
            flops=rows * width * tokens * 3, bytes_accessed=12 << 20, transcendentals=0
        ),
    )(places, starts, inverse, qd, delta, kv)


def local(queries, key_states, value_states, outputs, out_grad, doc_of_tile, tile_position):
    rows = queries.shape[0]
    kv_heads = key_states.shape[1] // HD
    head_count = lax.axis_size("head")
    ctx_count = lax.axis_size("ctx")
    ctx_index = lax.axis_index("ctx")
    split = kv_heads * head_count
    team = kv_heads
    near = [[b * team + s for s in range(team)] for b in range(ctx_count // team)]
    far = [[b * team + s for b in range(ctx_count // team)] for s in range(team)]

    def swap(value, split_axis, concat_axis):
        if head_count > 1:
            return lax.all_to_all(value, "head", split_axis, concat_axis, tiled=True)
        return lax.all_to_all(
            value, "ctx", split_axis, concat_axis, axis_index_groups=near, tiled=True
        )

    heads = queries.shape[1] // split // HD
    products = out_grad.astype(jnp.float32) * outputs.astype(jnp.float32)
    delta = jnp.sum(products.reshape(rows, split * heads, HD), axis=-1)
    if head_count == 1:
        kv = jnp.concatenate(
            [key_states.reshape(rows, split, HD), value_states.reshape(rows, split, HD)], axis=2
        ).reshape(rows, split * 2 * HD)
        kv = swap(kv, 1, 0)
    else:
        kv = jnp.concatenate([key_states, value_states], axis=1)
    kv_all = lax.all_gather(kv, "ctx", axis=0, tiled=True, axis_index_groups=far)
    qd = jnp.concatenate(
        [
            queries.reshape(rows, split, heads * HD),
            out_grad.reshape(rows, split, heads * HD),
        ],
        axis=2,
    ).reshape(rows, split * 2 * heads * HD)
    qd = swap(qd, 1, 0)
    delta = swap(delta, 1, 0)
    many = qd.shape[0]
    tiles = many // TILE
    delta = jnp.transpose(delta.reshape(tiles, TILE, heads), (0, 2, 1)).reshape(
        tiles, 1, heads * TILE
    )
    count = tile_position.shape[0]
    order = jnp.arange(count, dtype=jnp.int32)
    inverse = jnp.sum(
        jnp.where(tile_position[None, :] == order[:, None], order[None, :], 0), axis=1
    ).astype(jnp.int32)
    places = lax.dynamic_slice_in_dim(tile_position, (ctx_index // team) * tiles, tiles)
    starts = jnp.sum(
        (doc_of_tile[None, :] < doc_of_tile[places][:, None]).astype(jnp.int32), axis=1
    ).astype(jnp.int32)
    dq, dkv = attention_backward(places, starts, inverse, qd, delta, kv_all)
    dkv = lax.psum_scatter(
        dkv, "ctx", scatter_dimension=0, axis_index_groups=far, tiled=True
    ).astype(jnp.bfloat16)
    if head_count == 1:
        dq = swap(dq, 0, 1)
        dkv = swap(dkv, 0, 1)
    dkv = dkv.reshape(dkv.shape[0], kv_heads, 2, HD)
    width = kv_heads * HD
    return (
        dq,
        dkv[:, :, 0].reshape(-1, width),
        dkv[:, :, 1].reshape(-1, width),
    )


def solution(mesh):
    placed = (
        P(("ctx", "head"), None),
        P("ctx", "head"),
        P("ctx", "head"),
        P(("ctx", "head"), None),
        P(("ctx", "head"), None),
        P(),
        P(),
    )
    return jax.shard_map(
        local,
        mesh=mesh,
        in_specs=placed,
        out_specs=(P("ctx", "head"), P("ctx", "head"), P("ctx", "head")),
        check_vma=False,
    )
```

time: 1070 us -> 207 us (0.19)
  waiting for transfers between devices: 433 us -> 134 us
  other arithmetic: 229 us -> 5.78 us
  matrix products: 210 us -> 0 us
  local copies, waits for them, and re-layouts: 145 us -> 9.71 us
  loops' own time: 25.8 us -> 0 us
  Pallas kernels: 0 us -> 17.3 us
    ppermute x96 -> x0, waiting for transfers between devices: 377 us -> none  [passed_along(): return lax.ppermute(value, axis, pairs)]
    dot_general x192 -> x0, matrix products: 210 us -> none  [the longest x32 109 us: block_terms(): jnp.einsum('kgqp,pkd->qkgd', grad_scores, key_block, preferred_element_ty...]
    reduce_sum x163 -> x3, other arithmetic: 115 us -> 0.9 us  [the longest x1 0.61 us: local(): delta = jnp.sum(products.reshape(rows, split * heads, HD), axis=-1)]
    reduce_scatter x0 -> x1, waiting for transfers between devices: none -> 92.9 us  [local(): lax.psum_scatter(dkv, 'ctx', scatter_dimension=0, axis_index_groups=far,...]
    while x225 -> x0, local copies, waits for them, and re-layouts: 80.3 us -> none
    add x130 -> x0, other arithmetic: 63.4 us -> none  [the longest x32 60.9 us: turn(): key_grads = key_grads + key_term]
    dynamic_slice x64 -> x0, local copies, waits for them, and re-layouts: 48.2 us -> none  [the longest x32 29.5 us: absorb(): lax.dynamic_slice_in_dim(piece, begin, span, 0).reshape(span, kv_heads, HD)]
    and x64 -> x0, other arithmetic: 46.7 us -> none  [the longest x32 23.4 us: block_terms(): (query_doc[:, None] == key_doc[None, :]) & (key_pos[None, :] <= query_pos...]
  transfers between devices with their start and end apart: 97 -> 6, of which waited for: 65 -> 5; matrix products, arithmetic and copies ran while one was open for 11% -> 5% of each run, Pallas kernels for 0% -> 0%
where the time goes in v1:
time: 207 us; the launch traced here: 205 us
  waiting for transfers between devices  134 us (65%)
  Pallas kernels  17.3 us (8%)
  between operations  14.2 us (7%)
  starting transfers between devices  13.9 us (7%)
  blocking collectives  10.2 us (5%)
  local copies, waits for them, and re-layouts  9.71 us (5%)
  other arithmetic  5.78 us (3%)
    reduce_scatter x1, waiting for transfers between devices, local(): lax.psum_scatter(dkv, 'ctx', scatter_dimension=0, axis_index_groups=far,...  92.9 us
    all_to_all x4, waiting for transfers between devices, swap(): lax.all_to_all(value, 'ctx', split_axis, concat_axis, axis_index_groups=n...  30.4 us
    pallas_call x1, Pallas kernels, attention_backward(): pl.pallas_call(functools.partial(kernel, heads, tiles), out_shape=(jax.Sh...  17.3 us
    all_to_all x4, starting transfers between devices, swap(): lax.all_to_all(value, 'ctx', split_axis, concat_axis, axis_index_groups=n...  13.8 us
    all_gather x1, waiting for transfers between devices, local(): lax.all_gather(kv, 'ctx', axis=0, tiled=True, axis_index_groups=far)  10.6 us
    all_to_all x1, blocking collectives, swap(): lax.all_to_all(value, 'ctx', split_axis, concat_axis, axis_index_groups=n...  10.2 us
    unnamed x15, local copies, waits for them, and re-layouts  4.51 us
  transfers between devices with their start and end apart: 6, of which 5 were waited for; matrix products, arithmetic and copies ran while one was open for 5% of the time, Pallas kernels for 0%

profile of v1, /device:TPU:0, one launch (start us, length us, event | category | flops | bytes accessed | tf_op | source)
XLA Modules:
  0.0 204.9 jit_solution(16904636019655839112)
XLA Ops:
  7.2 0.0 copy-start
  7.2 0.0 copy-start.3
  7.2 0.0 all-gather.2.cloned.1.call-start
  7.2 0.8 copy-done
  8.1 0.9 copy_bitcast_fusion.4
  9.1 10.2 %all_to_all.80 = bf16[128,4,256]{2,0,1:T(8,128)(2,1)} all-to-all(bf16[128,4,256]{2,0,1:T(8,128)(2,1)S(1)} %pad_maximum_fusion.1), channel_id=1, replica_groups={{0,1,2,3},{4,5,6,7},{8,9,10,11},{12,13,14,15},{16,17,18,19},{20,21,22,2..., dimensions={1} | all-to-all | bytes 524288 | tf_op jit(solution)/shard_map/all_to_all | solution.py:169
  19.2 0.0 all-gather.2.cloned.1.call-update
  19.3 0.0 copy-done.3
  19.3 1.5 multiply_bitcast_fusion
  20.8 0.4 copy.55
  21.1 0.6 reduce_sum.29
  21.7 0.7 copy.42
  22.4 3.3 %all-to-all-start.1 = ((f32[128,4,8]{0,2,1:T(8,128)}), f32[128,4,8]{0,2,1:T(8,128)S(1)}, u32[]{:S(2)}, u32[]{:S(2)}) async-start(f32[128,4,8]{0,2,1:T(8,128)} %bitcast.2), calls=%async_computation.1 | async-start | bytes 32768 | tf_op jit(solution)/shard_map/all_to_all | solution.py:169
  25.7 1.4 copy_bitcast_fusion
  27.1 1.5 pad_maximum_fusion
  28.6 0.0 copy-start.4
  28.6 0.0 copy-start.2
  28.6 0.9 all-to-all-done.1
  29.5 3.6 %all-to-all-start = ((bf16[128,4,2048]{2,0,1:T(8,128)(2,1)}), bf16[128,4,2048]{2,0,1:T(8,128)(2,1)S(1)}, u32[]{:S(2)}, u32[]{:S(2)}) async-start(bf16[128,4,2048]{2,0,1:T(8,128)(2,1)} %pad_maximum_fusion), calls=%async_computation | async-start | bytes 4194304 | tf_op jit(solution)/shard_map/all_to_all | solution.py:169
  33.1 0.0 reduce-scatter.2.cloned.1.call-start
  33.2 0.0 copy-done.4
  33.2 0.1 compare_select_fusion
  33.3 0.0 copy-done.2
  33.3 0.6 gather_fusion
  33.9 0.1 select_reduce_fusion.inverse_ref
  34.0 0.2 convert_reduce_fusion.place_start_ref
  34.2 24.6 %all-to-all-done = bf16[128,4,2048]{2,0,1:T(8,128)(2,1)S(1)} async-done(((bf16[128,4,2048]{2,0,1:T(8,128)(2,1)}), bf16[128,4,2048]{2,0,1:T(8,128)(2,1)S(1)}, u32[]{:S(2)}, u32[]{:S(2)}) %all-to-all-start) | async-done | bytes 2097184 | tf_op jit(solution)/shard_map/all_to_all | solution.py:169
  58.8 10.6 %all-gather.2.cloned.1.call-done.kv_ref = bf16[4096,256]{1,0:T(8,128)(2,1)} async-done(((bf16[512,256]{1,0:T(8,128)(2,1)}), bf16[4096,256]{1,0:T(8,128)(2,1)}) %all-gather.2.cloned.1.call-update) | async-done | bytes 2097168 | tf_op jit(solution)/shard_map/all_gather | solution.py:183
  69.4 0.0 copy-start.1
  69.4 1.6 copy-done.1
  71.0 17.3 %shard_map.94 = (bf16[512,1024]{1,0:T(8,128)(2,1)}, f32[4096,256]{1,0:T(8,128)}) custom-call(s32[4]{0:T(128)S(1)} %get-tuple-element.8.place_ref, s32[4]{0:T(128)S(1)} %convert_reduce_fusion.place_start_ref, s32[32]{0:T(128)S(1)} %select_reduce_fusion.inverse_ref, bf16[512,2048]{1,0:T(8,128)(2,1)S(1)} %bitcast.49, f32[4,1,1024]{2,1,0:T(1,128)S(1)} %bitcast.50, ...), custom_call_target="tpu_custom_call" | custom-call | flops 6442450944 | bytes 12582912 | tf_op jit(solution)/shard_map/pallas_call | solution.py:132
  88.3 0.0 reduce-scatter.2.cloned.1.call-update
  88.3 3.5 %all-to-all-start.3 = ((bf16[4,128,1024]{2,1,0:T(8,128)(2,1)}), bf16[4,128,1024]{2,1,0:T(8,128)(2,1)S(1)}, u32[]{:S(2)}, u32[]{:S(2)}) async-start(bf16[4,128,1024]{2,1,0:T(8,128)(2,1)} %bitcast.7), calls=%async_computation.3 | async-start | bytes 2097152 | tf_op jit(solution)/shard_map/all_to_all | solution.py:169
  91.8 92.9 %reduce-scatter.2.cloned.1.call-done = f32[512,256]{1,0:T(8,128)} async-done(((f32[4096,256]{1,0:T(8,128)}), f32[512,256]{1,0:T(8,128)}) %reduce-scatter.2.cloned.1.call-update) | async-done | bytes 524304 | tf_op jit(solution)/shard_map/reduce_scatter | solution.py:208
  184.7 1.8 convert_element_type.15
  186.5 0.0 all-to-all-done.3
  186.5 3.4 %all-to-all-start.4 = ((bf16[4,128,256]{2,1,0:T(8,128)(2,1)}), bf16[4,128,256]{2,1,0:T(8,128)(2,1)S(1)}, u32[]{:S(2)}, u32[]{:S(2)}) async-start(bf16[4,128,256]{2,1,0:T(8,128)(2,1)} %bitcast.9), calls=%async_computation.5 | async-start | bytes 524288 | tf_op jit(solution)/shard_map/all_to_all | solution.py:169
  189.9 1.1 copy.54
  191.0 4.9 %all-to-all-done.4 = bf16[4,128,256]{2,1,0:T(8,128)(2,1)S(1)} async-done(((bf16[4,128,256]{2,1,0:T(8,128)(2,1)}), bf16[4,128,256]{2,1,0:T(8,128)(2,1)S(1)}, u32[]{:S(2)}, u32[]{:S(2)}) %all-to-all-start.4) | async-done | bytes 262176 | tf_op jit(solution)/shard_map/all_to_all | solution.py:169
  195.9 0.1 reshape.58
  196.0 0.4 fusion
  196.3 0.2 copy.49
  196.5 0.7 copy.64
  197.2 0.2 copy.48
  197.4 0.7 copy.65
  (2 shorter events, 0.0 us)
Async XLA Ops:
  7.2 0.9 copy-start
  7.2 12.1 %copy-start.3 = (bf16[128,4096]{1,0:T(8,128)(2,1)S(1)}, bf16[128,4096]{1,0:T(8,128)(2,1)}, u32[]{:S(2)}) copy-start(bf16[128,4096]{1,0:T(8,128)(2,1)} %param.11) | copy-start | bytes 3145732
  7.2 62.2 %all-gather.2.cloned.1.call-start = ((), (), s32[]{:S(2)}) async-start(), calls=%async_computation.6 | async-start | bytes 2359296 | tf_op jit(solution)/shard_map/all_gather | solution.py:183
  22.4 7.1 %all-to-all-start.1 = ((f32[128,4,8]{0,2,1:T(8,128)}), f32[128,4,8]{0,2,1:T(8,128)S(1)}, u32[]{:S(2)}, u32[]{:S(2)}) async-start(f32[128,4,8]{0,2,1:T(8,128)} %bitcast.2), calls=%async_computation.1 | async-start | bytes 32768 | tf_op jit(solution)/shard_map/all_to_all | solution.py:169
  28.6 4.6 %copy-start.4 = (s32[32]{0:T(128)S(1)}, s32[32]{0:T(128)}, u32[]{:S(2)}) copy-start(s32[32]{0:T(128)} %param.13) | copy-start | bytes 388
  28.6 4.7 %copy-start.2 = (s32[32]{0:T(128)S(1)}, s32[32]{0:T(128)}, u32[]{:S(2)}) copy-start(s32[32]{0:T(128)} %param.12) | copy-start | bytes 388
  29.5 29.3 %all-to-all-start = ((bf16[128,4,2048]{2,0,1:T(8,128)(2,1)}), bf16[128,4,2048]{2,0,1:T(8,128)(2,1)S(1)}, u32[]{:S(2)}, u32[]{:S(2)}) async-start(bf16[128,4,2048]{2,0,1:T(8,128)(2,1)} %pad_maximum_fusion), calls=%async_computation | async-start | bytes 4194304 | tf_op jit(solution)/shard_map/all_to_all | solution.py:169
  33.1 151.6 %reduce-scatter.2.cloned.1.call-start = ((), (), s32[]{:S(2)}) async-start(), calls=%async_computation.7 | async-start | bytes 4718592 | tf_op jit(solution)/shard_map/reduce_scatter | solution.py:208
  69.4 1.6 copy-start.1
  88.3 98.2 %all-to-all-start.3 = ((bf16[4,128,1024]{2,1,0:T(8,128)(2,1)}), bf16[4,128,1024]{2,1,0:T(8,128)(2,1)S(1)}, u32[]{:S(2)}, u32[]{:S(2)}) async-start(bf16[4,128,1024]{2,1,0:T(8,128)(2,1)} %bitcast.7), calls=%async_computation.3 | async-start | bytes 2097152 | tf_op jit(solution)/shard_map/all_to_all | solution.py:169
  186.5 9.4 %all-to-all-start.4 = ((bf16[4,128,256]{2,1,0:T(8,128)(2,1)}), bf16[4,128,256]{2,1,0:T(8,128)(2,1)S(1)}, u32[]{:S(2)}, u32[]{:S(2)}) async-start(bf16[4,128,256]{2,1,0:T(8,128)(2,1)} %bitcast.9), calls=%async_computation.5 | async-start | bytes 524288 | tf_op jit(solution)/shard_map/all_to_all | solution.py:169
Sparse Core Ops, SparseCore 0:
  19.4 49.9 all-gather.1
  88.4 96.2 reduce-scatter.1

commit v2 on v1

--- a/solution.py
+++ b/solution.py
@@ -30,11 +30,12 @@
     g_cols,
     score_buf,
     dq_acc,
+    dkv_acc,
 ):
     width = heads * HD
     scale = HD ** (-0.5)
     keys = SPAN * TILE
-    dkv_ref[...] = jnp.zeros_like(dkv_ref)
+    dkv_acc[...] = jnp.zeros_like(dkv_acc)
     row_id = lax.broadcasted_iota(jnp.int32, (keys, width), 0)
     col_id = lax.broadcasted_iota(jnp.int32, (keys, width), 1) & (TILE - 1)
     gap = row_id - col_id
@@ -112,12 +113,14 @@
             )
             for offset, spot in enumerate(spots(last)):
                 rows = slice(offset * TILE, (offset + 1) * TILE)
-                dkv_ref[pl.ds(spot, TILE), 0:HD] += dk[rows]
-                dkv_ref[pl.ds(spot, TILE), HD : 2 * HD] += dv[rows]
+                dkv_acc[pl.ds(spot, TILE), 0:HD] += dk[rows]
+                dkv_acc[pl.ds(spot, TILE), HD : 2 * HD] += dv[rows]
 
         for h in range(heads):
             lanes = slice(h * HD, (h + 1) * HD)
             dq_ref[pl.ds(first_row, TILE), lanes] = dq_acc[:, lanes].T.astype(jnp.bfloat16)
+
+    dkv_ref[...] = dkv_acc[...].astype(jnp.bfloat16)
 
 
 def attention_backward(places, starts, inverse, qd, delta, kv):
@@ -133,7 +136,7 @@
         functools.partial(kernel, heads, tiles),
         out_shape=(
             jax.ShapeDtypeStruct((rows, width), jnp.bfloat16),
-            jax.ShapeDtypeStruct((tokens, 2 * HD), jnp.float32),
+            jax.ShapeDtypeStruct((tokens, 2 * HD), jnp.bfloat16),
         ),
         in_specs=[smem, smem, smem, vmem, vmem, vmem],
         out_specs=(vmem, vmem),
@@ -144,6 +147,7 @@
             pltpu.VMEM((HD, width), jnp.bfloat16),
             pltpu.VMEM((steps // 2 + 1, SPAN * TILE, width), jnp.float32),
             pltpu.VMEM((HD, width), jnp.float32),
+            pltpu.VMEM((tokens, 2 * HD), jnp.float32),
         ],
         compiler_params=pltpu.CompilerParams(vmem_limit_bytes=48 * 1024 * 1024),
         cost_estimate=pl.CostEstimate(
@@ -205,9 +209,9 @@
         (doc_of_tile[None, :] < doc_of_tile[places][:, None]).astype(jnp.int32), axis=1
     ).astype(jnp.int32)
     dq, dkv = attention_backward(places, starts, inverse, qd, delta, kv_all)
-    dkv = lax.psum_scatter(
-        dkv, "ctx", scatter_dimension=0, axis_index_groups=far, tiled=True
-    ).astype(jnp.bfloat16)
+    parts = ctx_count // team
+    dkv = lax.all_to_all(dkv, "ctx", 0, 0, axis_index_groups=far, tiled=True)
+    dkv = jnp.sum(dkv.reshape(parts, -1, 2 * HD).astype(jnp.float32), axis=0).astype(jnp.bfloat16)
     if head_count == 1:
         dq = swap(dq, 0, 1)
         dkv = swap(dkv, 0, 1)

time: 207 us -> 185 us (0.89)
  waiting for transfers between devices: 134 us -> 54.5 us
  blocking collectives: 10.2 us -> 60.1 us
  Pallas kernels: 17.3 us -> 29.5 us
    reduce_scatter x1 -> x0, waiting for transfers between devices: 92.9 us -> none  [local(): lax.psum_scatter(dkv, 'ctx', scatter_dimension=0, axis_index_groups=far,...]
    all_to_all x0 -> x1, blocking collectives: none -> 49.9 us  [local(): dkv = lax.all_to_all(dkv, 'ctx', 0, 0, axis_index_groups=far, tiled=True)]
    all_to_all x4, waiting for transfers between devices: 30.4 us -> 43.8 us  [swap(): lax.all_to_all(value, 'ctx', split_axis, concat_axis, axis_index_groups=n...]
    pallas_call x1, Pallas kernels: 17.3 us -> 29.5 us  [attention_backward(): pl.pallas_call(functools.partial(kernel, heads, tiles), out_shape=(jax.Sh...]
    unnamed x15 -> x11, local copies, waits for them, and re-layouts: 4.51 us -> 2.77 us
  transfers between devices with their start and end apart: 6 -> 5, of which waited for: 5 -> 5; matrix products, arithmetic and copies ran while one was open for 5% -> 5% of each run, Pallas kernels for 0% -> 0%
where the time goes in v2:
time: 185 us
  blocking collectives  60.1 us (32%)
  waiting for transfers between devices  54.5 us (29%)
  Pallas kernels  29.5 us (16%)
  between operations  14.2 us (8%)
  starting transfers between devices  13.8 us (7%)
  local copies, waits for them, and re-layouts  7.72 us (4%)
  other arithmetic  5.03 us (3%)
    all_to_all x1, blocking collectives, local(): dkv = lax.all_to_all(dkv, 'ctx', 0, 0, axis_index_groups=far, tiled=True)  49.9 us
    all_to_all x4, waiting for transfers between devices, swap(): lax.all_to_all(value, 'ctx', split_axis, concat_axis, axis_index_groups=n...  43.8 us
    pallas_call x1, Pallas kernels, attention_backward(): pl.pallas_call(functools.partial(kernel, heads, tiles), out_shape=(jax.Sh...  29.5 us
    all_to_all x4, starting transfers between devices, swap(): lax.all_to_all(value, 'ctx', split_axis, concat_axis, axis_index_groups=n...  13.8 us
    all_gather x1, waiting for transfers between devices, local(): lax.all_gather(kv, 'ctx', axis=0, tiled=True, axis_index_groups=far)  10.6 us
    all_to_all x1, blocking collectives, swap(): lax.all_to_all(value, 'ctx', split_axis, concat_axis, axis_index_groups=n...  10.2 us
  transfers between devices with their start and end apart: 5, of which 5 were waited for; matrix products, arithmetic and copies ran while one was open for 5% of the time, Pallas kernels for 0%

profile of v2, /device:TPU:0, one launch (start us, length us, event | category | flops | bytes accessed | tf_op | source)
XLA Modules:
  0.0 184.8 jit_solution(2412749834322045632)
XLA Ops:
  7.2 0.0 copy-start
  7.2 0.0 copy-start.2
  7.2 0.0 all-gather.2.cloned.1.call-start
  7.2 0.8 copy-done
  8.1 0.9 copy_bitcast_fusion.2
  9.1 10.2 %all_to_all.89 = bf16[128,4,256]{2,0,1:T(8,128)(2,1)} all-to-all(bf16[128,4,256]{2,0,1:T(8,128)(2,1)S(1)} %pad_maximum_fusion.1), channel_id=1, replica_groups={{0,1,2,3},{4,5,6,7},{8,9,10,11},{12,13,14,15},{16,17,18,19},{20,21,22,2..., dimensions={1} | all-to-all | bytes 524288 | tf_op jit(solution)/shard_map/all_to_all | solution.py:173
  19.2 0.0 all-gather.2.cloned.1.call-update
  19.3 0.0 copy-done.2
  19.3 1.5 multiply_bitcast_fusion
  20.8 0.4 copy.62
  21.1 0.6 reduce_sum.41
  21.7 0.7 copy.50
  22.4 3.3 %all-to-all-start.1 = ((f32[128,4,8]{0,2,1:T(8,128)}), f32[128,4,8]{0,2,1:T(8,128)S(1)}, u32[]{:S(2)}, u32[]{:S(2)}) async-start(f32[128,4,8]{0,2,1:T(8,128)} %bitcast.2), calls=%async_computation.1 | async-start | bytes 32768 | tf_op jit(solution)/shard_map/all_to_all | solution.py:173
  25.7 1.4 copy_bitcast_fusion
  27.1 1.5 pad_maximum_fusion
  28.6 0.0 copy-start.3
  28.6 0.0 copy-start.1
  28.6 0.9 all-to-all-done.1
  29.5 3.6 %all-to-all-start = ((bf16[128,4,2048]{2,0,1:T(8,128)(2,1)}), bf16[128,4,2048]{2,0,1:T(8,128)(2,1)S(1)}, u32[]{:S(2)}, u32[]{:S(2)}) async-start(bf16[128,4,2048]{2,0,1:T(8,128)(2,1)} %pad_maximum_fusion), calls=%async_computation | async-start | bytes 4194304 | tf_op jit(solution)/shard_map/all_to_all | solution.py:173
  33.1 0.0 copy-done.3
  33.2 0.1 compare_select_fusion
  33.2 0.0 copy-done.1
  33.2 0.6 gather_fusion
  33.9 0.1 select_reduce_fusion.inverse_ref
  34.0 0.2 convert_reduce_fusion.place_start_ref
  34.2 24.6 %all-to-all-done = bf16[128,4,2048]{2,0,1:T(8,128)(2,1)S(1)} async-done(((bf16[128,4,2048]{2,0,1:T(8,128)(2,1)}), bf16[128,4,2048]{2,0,1:T(8,128)(2,1)S(1)}, u32[]{:S(2)}, u32[]{:S(2)}) %all-to-all-start) | async-done | bytes 2097184 | tf_op jit(solution)/shard_map/all_to_all | solution.py:173
  58.8 10.6 %all-gather.2.cloned.1.call-done.kv_ref = bf16[4096,256]{1,0:T(8,128)(2,1)} async-done(((bf16[512,256]{1,0:T(8,128)(2,1)}), bf16[4096,256]{1,0:T(8,128)(2,1)}) %all-gather.2.cloned.1.call-update) | async-done | bytes 2097168 | tf_op jit(solution)/shard_map/all_gather | solution.py:187
  69.4 29.5 %shard_map.94 = (bf16[512,1024]{1,0:T(8,128)(2,1)}, bf16[4096,256]{1,0:T(8,128)(2,1)S(1)}) custom-call(s32[4]{0:T(128)S(1)} %get-tuple-element.23.place_ref, s32[4]{0:T(128)S(1)} %convert_reduce_fusion.place_start_ref, s32[32]{0:T(128)S(1)} %select_reduce_fusion.inverse_ref, bf16[512,2048]{1,0:T(8,128)(2,1)S(1)} %bitcast.39, f32[4,1,1024]{2,1,0:T(1,128)S(1)} %bitcast.41, ...), custom_call_target="tpu_custom_call" | custom-call | flops 6442450944 | bytes 12582912 | tf_op jit(solution)/shard_map/pallas_call | solution.py:135
  98.9 49.9 %all_to_all.90 = bf16[8,512,256]{2,1,0:T(8,128)(2,1)S(1)} all-to-all(bf16[8,512,256]{2,1,0:T(8,128)(2,1)S(1)} %bitcast.40), channel_id=1, replica_groups={{0,4,8,12,16,20,24,28},{1,5,9,13,17,21,25,29},{2,6,10,14,18,22,26,30},{..., dimensions={0} | all-to-all | bytes 4194304 | tf_op jit(solution)/shard_map/all_to_all | solution.py:213
  148.9 3.5 %all-to-all-start.3 = ((bf16[4,128,1024]{2,1,0:T(8,128)(2,1)}), bf16[4,128,1024]{2,1,0:T(8,128)(2,1)S(1)}, u32[]{:S(2)}, u32[]{:S(2)}) async-start(bf16[4,128,1024]{2,1,0:T(8,128)(2,1)} %bitcast.7), calls=%async_computation.3 | async-start | bytes 2097152 | tf_op jit(solution)/shard_map/all_to_all | solution.py:173
  152.4 1.0 reduce_sum.42
  153.4 13.4 %all-to-all-done.3 = bf16[4,128,1024]{2,1,0:T(8,128)(2,1)S(1)} async-done(((bf16[4,128,1024]{2,1,0:T(8,128)(2,1)}), bf16[4,128,1024]{2,1,0:T(8,128)(2,1)S(1)}, u32[]{:S(2)}, u32[]{:S(2)}) %all-to-all-start.3) | async-done | bytes 1048608 | tf_op jit(solution)/shard_map/all_to_all | solution.py:173
  166.8 3.4 %all-to-all-start.5 = ((bf16[4,128,256]{2,1,0:T(8,128)(2,1)}), bf16[4,128,256]{2,1,0:T(8,128)(2,1)S(1)}, u32[]{:S(2)}, u32[]{:S(2)}) async-start(bf16[4,128,256]{2,1,0:T(8,128)(2,1)} %bitcast.10), calls=%async_computation.5 | async-start | bytes 524288 | tf_op jit(solution)/shard_map/all_to_all | solution.py:173
  170.2 1.1 copy.61
  171.3 4.9 %all-to-all-done.5 = bf16[4,128,256]{2,1,0:T(8,128)(2,1)S(1)} async-done(((bf16[4,128,256]{2,1,0:T(8,128)(2,1)}), bf16[4,128,256]{2,1,0:T(8,128)(2,1)S(1)}, u32[]{:S(2)}, u32[]{:S(2)}) %all-to-all-start.5) | async-done | bytes 262176 | tf_op jit(solution)/shard_map/all_to_all | solution.py:173
  176.2 0.2 copy.54
  176.4 0.8 copy.56
  177.2 0.8 copy.55
  (3 shorter events, 0.1 us)
Async XLA Ops:
  7.2 0.9 copy-start
  7.2 12.1 %copy-start.2 = (bf16[128,4096]{1,0:T(8,128)(2,1)S(1)}, bf16[128,4096]{1,0:T(8,128)(2,1)}, u32[]{:S(2)}) copy-start(bf16[128,4096]{1,0:T(8,128)(2,1)} %param.11) | copy-start | bytes 3145732
  7.2 62.2 %all-gather.2.cloned.1.call-start = ((), (), s32[]{:S(2)}) async-start(), calls=%async_computation.6 | async-start | bytes 2359296 | tf_op jit(solution)/shard_map/all_gather | solution.py:187
  22.4 7.1 %all-to-all-start.1 = ((f32[128,4,8]{0,2,1:T(8,128)}), f32[128,4,8]{0,2,1:T(8,128)S(1)}, u32[]{:S(2)}, u32[]{:S(2)}) async-start(f32[128,4,8]{0,2,1:T(8,128)} %bitcast.2), calls=%async_computation.1 | async-start | bytes 32768 | tf_op jit(solution)/shard_map/all_to_all | solution.py:173
  28.6 4.5 %copy-start.3 = (s32[32]{0:T(128)S(1)}, s32[32]{0:T(128)}, u32[]{:S(2)}) copy-start(s32[32]{0:T(128)} %param.13) | copy-start | bytes 388
  28.6 4.6 %copy-start.1 = (s32[32]{0:T(128)S(1)}, s32[32]{0:T(128)}, u32[]{:S(2)}) copy-start(s32[32]{0:T(128)} %param.12) | copy-start | bytes 388
  29.5 29.3 %all-to-all-start = ((bf16[128,4,2048]{2,0,1:T(8,128)(2,1)}), bf16[128,4,2048]{2,0,1:T(8,128)(2,1)S(1)}, u32[]{:S(2)}, u32[]{:S(2)}) async-start(bf16[128,4,2048]{2,0,1:T(8,128)(2,1)} %pad_maximum_fusion), calls=%async_computation | async-start | bytes 4194304 | tf_op jit(solution)/shard_map/all_to_all | solution.py:173
  148.9 18.0 %all-to-all-start.3 = ((bf16[4,128,1024]{2,1,0:T(8,128)(2,1)}), bf16[4,128,1024]{2,1,0:T(8,128)(2,1)S(1)}, u32[]{:S(2)}, u32[]{:S(2)}) async-start(bf16[4,128,1024]{2,1,0:T(8,128)(2,1)} %bitcast.7), calls=%async_computation.3 | async-start | bytes 2097152 | tf_op jit(solution)/shard_map/all_to_all | solution.py:173
  166.8 9.4 %all-to-all-start.5 = ((bf16[4,128,256]{2,1,0:T(8,128)(2,1)}), bf16[4,128,256]{2,1,0:T(8,128)(2,1)S(1)}, u32[]{:S(2)}, u32[]{:S(2)}) async-start(bf16[4,128,256]{2,1,0:T(8,128)(2,1)} %bitcast.10), calls=%async_computation.5 | async-start | bytes 524288 | tf_op jit(solution)/shard_map/all_to_all | solution.py:173
Sparse Core Ops, SparseCore 0:
  19.4 49.9 all-gather.1

commit v3 on v2

--- a/solution.py
+++ b/solution.py
@@ -210,11 +210,22 @@
     ).astype(jnp.int32)
     dq, dkv = attention_backward(places, starts, inverse, qd, delta, kv_all)
     parts = ctx_count // team
+    if head_count == 1:
+        blocks = dq.reshape(team, rows, -1)
+        me = ctx_index & (team - 1)
+        home = jnp.zeros_like(blocks)
+        for shift in range(team):
+            piece = lax.dynamic_index_in_dim(blocks, me ^ shift, 0)
+            if shift:
+                pairs = [(i, i ^ shift) for i in range(ctx_count)]
+                piece = lax.ppermute(piece, "ctx", pairs)
+            home = lax.dynamic_update_slice_in_dim(home, piece, me ^ shift, 0)
+        dq_home = jnp.transpose(home, (1, 0, 2)).reshape(rows, -1)
     dkv = lax.all_to_all(dkv, "ctx", 0, 0, axis_index_groups=far, tiled=True)
     dkv = jnp.sum(dkv.reshape(parts, -1, 2 * HD).astype(jnp.float32), axis=0).astype(jnp.bfloat16)
     if head_count == 1:
-        dq = swap(dq, 0, 1)
         dkv = swap(dkv, 0, 1)
+        dq = dq_home
     dkv = dkv.reshape(dkv.shape[0], kv_heads, 2, HD)
     width = kv_heads * HD
     return (

time: 185 us -> 180 us (0.973)
  blocking collectives: 60.1 us -> 10.2 us
  waiting for transfers between devices: 54.5 us -> 80.7 us
  local copies, waits for them, and re-layouts: 7.72 us -> 25.9 us
  starting transfers between devices: 13.8 us -> 15.8 us
    all_to_all x1 -> x0, blocking collectives: 49.9 us -> none  [local(): dkv = lax.all_to_all(dkv, 'ctx', 0, 0, axis_index_groups=far, tiled=True)]
    all_to_all x0 -> x1, waiting for transfers between devices: none -> 44.6 us  [local(): dkv = lax.all_to_all(dkv, 'ctx', 0, 0, axis_index_groups=far, tiled=True)]
    all_to_all x4 -> x3, waiting for transfers between devices: 43.8 us -> 25.5 us  [swap(): lax.all_to_all(value, 'ctx', split_axis, concat_axis, axis_index_groups=n...]
    dynamic_update_slice x0 -> x4, local copies, waits for them, and re-layouts: none -> 13.7 us  [local(): home = lax.dynamic_update_slice_in_dim(home, piece, me ^ shift, 0)]
    all_to_all x0 -> x1, starting transfers between devices: none -> 3.6 us  [local(): dkv = lax.all_to_all(dkv, 'ctx', 0, 0, axis_index_groups=far, tiled=True)]
    all_to_all x4 -> x3, starting transfers between devices: 13.8 us -> 10.3 us  [swap(): lax.all_to_all(value, 'ctx', split_axis, concat_axis, axis_index_groups=n...]
    unnamed x11 -> x14, local copies, waits for them, and re-layouts: 2.77 us -> 5.42 us
    ppermute x0 -> x3, starting transfers between devices: none -> 1.86 us  [local(): piece = lax.ppermute(piece, 'ctx', pairs)]
  transfers between devices with their start and end apart: 5 -> 8, of which waited for: 5 -> 4; matrix products, arithmetic and copies ran while one was open for 5% -> 14% of each run, Pallas kernels for 0% -> 0%
where the time goes in v3:
time: 180 us
  waiting for transfers between devices  80.7 us (45%)
  Pallas kernels  28.6 us (16%)
  local copies, waits for them, and re-layouts  25.9 us (14%)
  starting transfers between devices  15.8 us (9%)
  between operations  14.3 us (8%)
  blocking collectives  10.2 us (6%)
  other arithmetic  5.04 us (3%)
    all_to_all x1, waiting for transfers between devices, local(): dkv = lax.all_to_all(dkv, 'ctx', 0, 0, axis_index_groups=far, tiled=True)  44.6 us
    pallas_call x1, Pallas kernels, attention_backward(): pl.pallas_call(functools.partial(kernel, heads, tiles), out_shape=(jax.Sh...  28.6 us
    all_to_all x3, waiting for transfers between devices, swap(): lax.all_to_all(value, 'ctx', split_axis, concat_axis, axis_index_groups=n...  25.5 us
    dynamic_update_slice x4, local copies, waits for them, and re-layouts, local(): home = lax.dynamic_update_slice_in_dim(home, piece, me ^ shift, 0)  13.7 us
    all_gather x1, waiting for transfers between devices, local(): lax.all_gather(kv, 'ctx', axis=0, tiled=True, axis_index_groups=far)  10.6 us
    all_to_all x3, starting transfers between devices, swap(): lax.all_to_all(value, 'ctx', split_axis, concat_axis, axis_index_groups=n...  10.3 us
    all_to_all x1, blocking collectives, swap(): lax.all_to_all(value, 'ctx', split_axis, concat_axis, axis_index_groups=n...  10.2 us
    unnamed x14, local copies, waits for them, and re-layouts  5.42 us
  transfers between devices with their start and end apart: 8, of which 4 were waited for; matrix products, arithmetic and copies ran while one was open for 14% of the time, Pallas kernels for 0%

profile of v3, /device:TPU:0, one launch (start us, length us, event | category | flops | bytes accessed | tf_op | source)
XLA Modules:
  0.0 180.4 jit_solution(4334577511308841087)
XLA Ops:
  7.2 0.0 copy-start
  7.2 0.0 copy-start.3
  7.2 0.0 all-gather.2.cloned.1.call-start
  7.2 0.8 copy-done
  8.1 0.9 copy_bitcast_fusion.2
  9.1 10.2 %all_to_all.70 = bf16[128,4,256]{2,0,1:T(8,128)(2,1)} all-to-all(bf16[128,4,256]{2,0,1:T(8,128)(2,1)S(1)} %pad_maximum_fusion.1), channel_id=1, replica_groups={{0,1,2,3},{4,5,6,7},{8,9,10,11},{12,13,14,15},{16,17,18,19},{20,21,22,2..., dimensions={1} | all-to-all | bytes 524288 | tf_op jit(solution)/shard_map/all_to_all | solution.py:173
  19.2 0.0 all-gather.2.cloned.1.call-update
  19.3 0.0 copy-done.3
  19.3 1.5 multiply_bitcast_fusion
  20.8 0.4 copy.79
  21.1 0.6 reduce_sum.41
  21.7 0.7 copy.65
  22.4 3.3 %all-to-all-start.1 = ((f32[128,4,8]{0,2,1:T(8,128)}), f32[128,4,8]{0,2,1:T(8,128)S(1)}, u32[]{:S(2)}, u32[]{:S(2)}) async-start(f32[128,4,8]{0,2,1:T(8,128)} %bitcast.2), calls=%async_computation.1 | async-start | bytes 32768 | tf_op jit(solution)/shard_map/all_to_all | solution.py:173
  25.7 1.4 copy_bitcast_fusion
  27.1 1.5 pad_maximum_fusion
  28.6 0.0 copy-start.4
  28.6 0.0 copy-start.2
  28.6 0.9 all-to-all-done.1
  29.5 3.6 %all-to-all-start = ((bf16[128,4,2048]{2,0,1:T(8,128)(2,1)}), bf16[128,4,2048]{2,0,1:T(8,128)(2,1)S(1)}, u32[]{:S(2)}, u32[]{:S(2)}) async-start(bf16[128,4,2048]{2,0,1:T(8,128)(2,1)} %pad_maximum_fusion), calls=%async_computation | async-start | bytes 4194304 | tf_op jit(solution)/shard_map/all_to_all | solution.py:173
  33.1 0.0 copy-done.4
  33.2 0.1 compare_select_fusion
  33.2 0.0 copy-done.2
  33.2 0.6 gather_fusion
  33.9 0.1 select_reduce_fusion.inverse_ref
  34.0 0.2 convert_reduce_fusion.place_start_ref
  34.2 24.6 %all-to-all-done = bf16[128,4,2048]{2,0,1:T(8,128)(2,1)S(1)} async-done(((bf16[128,4,2048]{2,0,1:T(8,128)(2,1)}), bf16[128,4,2048]{2,0,1:T(8,128)(2,1)S(1)}, u32[]{:S(2)}, u32[]{:S(2)}) %all-to-all-start) | async-done | bytes 2097184 | tf_op jit(solution)/shard_map/all_to_all | solution.py:173
  58.8 10.6 %all-gather.2.cloned.1.call-done.kv_ref = bf16[4096,256]{1,0:T(8,128)(2,1)} async-done(((bf16[512,256]{1,0:T(8,128)(2,1)}), bf16[4096,256]{1,0:T(8,128)(2,1)}) %all-gather.2.cloned.1.call-update) | async-done | bytes 2097168 | tf_op jit(solution)/shard_map/all_gather | solution.py:187
  69.4 28.6 %shard_map.94 = (bf16[512,1024]{1,0:T(8,128)(2,1)S(1)}, bf16[4096,256]{1,0:T(8,128)(2,1)S(1)}) custom-call(s32[4]{0:T(128)S(1)} %get-tuple-element.23.place_ref, s32[4]{0:T(128)S(1)} %convert_reduce_fusion.place_start_ref, s32[32]{0:T(128)S(1)} %select_reduce_fusion.inverse_ref, bf16[512,2048]{1,0:T(8,128)(2,1)S(1)} %bitcast.39, f32[4,1,1024]{2,1,0:T(1,128)S(1)} %bitcast.42, ...), custom_call_target="tpu_custom_call" | custom-call | flops 6442450944 | bytes 12582912 | tf_op jit(solution)/shard_map/pallas_call | solution.py:135
  98.0 0.0 copy-start.1
  98.1 1.3 copy-done.1
  99.4 3.6 %all-to-all-start.3 = ((bf16[8,512,256]{2,1,0:T(8,128)(2,1)}), bf16[8,512,256]{2,1,0:T(8,128)(2,1)S(1)}, u32[]{:S(2)}, u32[]{:S(2)}) async-start(bf16[8,512,256]{2,1,0:T(8,128)(2,1)} %bitcast.40), calls=%async_computation.3 | async-start | bytes 4194304 | tf_op jit(solution)/shard_map/all_to_all | solution.py:224
  103.0 0.9 constant_dynamic-slice_fusion
  103.9 0.0 collective-permute-start
  103.9 1.5 collective-permute-start.1
  105.4 0.4 collective-permute-start.2
  105.8 44.6 %all-to-all-done.3 = bf16[8,512,256]{2,1,0:T(8,128)(2,1)S(1)} async-done(((bf16[8,512,256]{2,1,0:T(8,128)(2,1)}), bf16[8,512,256]{2,1,0:T(8,128)(2,1)S(1)}, u32[]{:S(2)}, u32[]{:S(2)}) %all-to-all-start.3) | async-done | bytes 2097184 | tf_op jit(solution)/shard_map/all_to_all | solution.py:224
  150.3 1.0 reduce_sum.42
  151.4 3.4 %all-to-all-start.4 = ((bf16[4,128,256]{2,1,0:T(8,128)(2,1)}), bf16[4,128,256]{2,1,0:T(8,128)(2,1)S(1)}, u32[]{:S(2)}, u32[]{:S(2)}) async-start(bf16[4,128,256]{2,1,0:T(8,128)(2,1)} %bitcast.10), calls=%async_computation.4 | async-start | bytes 524288 | tf_op jit(solution)/shard_map/all_to_all | solution.py:173
  154.8 0.4 copy.68
  155.2 0.3 broadcast_in_dim.23
  155.5 3.4 %dynamic_update_slice.12 = bf16[4,128,1024]{2,0,1:T(4,128)(2,1)S(1)} dynamic-update-slice(bf16[4,128,1024]{2,0,1:T(4,128)(2,1)S(1)} %broadcast_in_dim.23, bf16[1,128,1024]{2,0,1:T(2,128)(2,1)S(1)} %copy.68, s32[]{:T(128)S(6)} %select_n.36, s32[]{:T(128)} %constant.37.clone.1, s32[]{:T(128)} %constant.37.clone.1) | dynamic-update-slice | bytes 524292 | tf_op jit(solution)/shard_map/dynamic_update_slice | solution.py:222
  158.9 0.0 collective-permute-done
  158.9 0.4 copy.69
  159.3 3.4 %dynamic_update_slice.13 = bf16[4,128,1024]{2,0,1:T(4,128)(2,1)S(1)} dynamic-update-slice(bf16[4,128,1024]{2,0,1:T(4,128)(2,1)S(1)} %dynamic_update_slice.12, bf16[1,128,1024]{2,0,1:T(2,128)(2,1)S(1)} %copy.69, s32[]{:T(128)S(6)} %select_n.37, s32[]{:T(128)} %constant.37.clone.1, s32[]{:T(128)} %constant.37.clone.1) | dynamic-update-slice | bytes 524292 | tf_op jit(solution)/shard_map/dynamic_update_slice | solution.py:222
  162.8 0.0 collective-permute-done.1
  162.8 0.4 copy.70
  163.2 3.4 %dynamic_update_slice.14 = bf16[4,128,1024]{2,0,1:T(4,128)(2,1)S(1)} dynamic-update-slice(bf16[4,128,1024]{2,0,1:T(4,128)(2,1)S(1)} %dynamic_update_slice.13, bf16[1,128,1024]{2,0,1:T(2,128)(2,1)S(1)} %copy.70, s32[]{:T(128)S(6)} %select_n.38, s32[]{:T(128)} %constant.37.clone.1, s32[]{:T(128)} %constant.37.clone.1) | dynamic-update-slice | bytes 524292 | tf_op jit(solution)/shard_map/dynamic_update_slice | solution.py:222
  166.6 0.0 collective-permute-done.2
  166.7 0.4 copy.71
  167.1 3.4 %dynamic_update_slice.15 = bf16[4,128,1024]{2,0,1:T(4,128)(2,1)S(1)} dynamic-update-slice(bf16[4,128,1024]{2,0,1:T(4,128)(2,1)S(1)} %dynamic_update_slice.14, bf16[1,128,1024]{2,0,1:T(2,128)(2,1)S(1)} %copy.71, s32[]{:T(128)S(6)} %select_n.39, s32[]{:T(128)} %constant.37.clone.1, s32[]{:T(128)} %constant.37.clone.1) | dynamic-update-slice | bytes 524292 | tf_op jit(solution)/shard_map/dynamic_update_slice | solution.py:222
  170.5 1.3 copy.80
  171.8 0.0 all-to-all-done.4
  171.8 0.2 copy.72
  172.1 0.8 copy.73
  172.8 0.8 copy.74
  (3 shorter events, 0.1 us)
Async XLA Ops:
  7.2 0.9 copy-start
  7.2 12.1 %copy-start.3 = (bf16[128,4096]{1,0:T(8,128)(2,1)S(1)}, bf16[128,4096]{1,0:T(8,128)(2,1)}, u32[]{:S(2)}) copy-start(bf16[128,4096]{1,0:T(8,128)(2,1)} %param.11) | copy-start | bytes 3145732
  7.2 62.2 %all-gather.2.cloned.1.call-start = ((), (), s32[]{:S(2)}) async-start(), calls=%async_computation.5 | async-start | bytes 2359296 | tf_op jit(solution)/shard_map/all_gather | solution.py:187
  22.4 7.1 %all-to-all-start.1 = ((f32[128,4,8]{0,2,1:T(8,128)}), f32[128,4,8]{0,2,1:T(8,128)S(1)}, u32[]{:S(2)}, u32[]{:S(2)}) async-start(f32[128,4,8]{0,2,1:T(8,128)} %bitcast.2), calls=%async_computation.1 | async-start | bytes 32768 | tf_op jit(solution)/shard_map/all_to_all | solution.py:173
  28.6 4.5 %copy-start.4 = (s32[32]{0:T(128)S(1)}, s32[32]{0:T(128)}, u32[]{:S(2)}) copy-start(s32[32]{0:T(128)} %param.13) | copy-start | bytes 388
  28.6 4.6 %copy-start.2 = (s32[32]{0:T(128)S(1)}, s32[32]{0:T(128)}, u32[]{:S(2)}) copy-start(s32[32]{0:T(128)} %param.12) | copy-start | bytes 388
  29.5 29.3 %all-to-all-start = ((bf16[128,4,2048]{2,0,1:T(8,128)(2,1)}), bf16[128,4,2048]{2,0,1:T(8,128)(2,1)S(1)}, u32[]{:S(2)}, u32[]{:S(2)}) async-start(bf16[128,4,2048]{2,0,1:T(8,128)(2,1)} %pad_maximum_fusion), calls=%async_computation | async-start | bytes 4194304 | tf_op jit(solution)/shard_map/all_to_all | solution.py:173
  98.0 1.3 copy-start.1
  99.4 50.9 %all-to-all-start.3 = ((bf16[8,512,256]{2,1,0:T(8,128)(2,1)}), bf16[8,512,256]{2,1,0:T(8,128)(2,1)S(1)}, u32[]{:S(2)}, u32[]{:S(2)}) async-start(bf16[8,512,256]{2,1,0:T(8,128)(2,1)} %bitcast.40), calls=%async_computation.3 | async-start | bytes 4194304 | tf_op jit(solution)/shard_map/all_to_all | solution.py:224
  103.9 55.0 %collective-permute-start = (bf16[1,128,1024]{2,1,0:T(8,128)(2,1)}, bf16[1,128,1024]{2,1,0:T(8,128)(2,1)S(1)}, u32[]{:S(2)}, u32[]{:S(2)}) collective-permute-start(bf16[1,128,1024]{2,1,0:T(8,128)(2,1)} %get-tuple-element.26), channel_id=1, source_target_pairs={{0,1},{1,0},{2,3},{3,2},{4,5},{5,4},{6,7},{7,6},{8,9},{9,8},{10,11... | collective-permute-start | bytes 786440 | tf_op jit(solution)/shard_map/ppermute | solution.py:221
  103.9 58.9 %collective-permute-start.1 = (bf16[1,128,1024]{2,1,0:T(8,128)(2,1)}, bf16[1,128,1024]{2,1,0:T(8,128)(2,1)S(1)}, u32[]{:S(2)}, u32[]{:S(2)}) collective-permute-start(bf16[1,128,1024]{2,1,0:T(8,128)(2,1)} %get-tuple-element.25), channel_id=1, source_target_pairs={{0,2},{1,3},{2,0},{3,1},{4,6},{5,7},{6,4},{7,5},{8,10},{9,11},{10,... | collective-permute-start | bytes 786440 | tf_op jit(solution)/shard_map/ppermute | solution.py:221
  105.4 61.3 %collective-permute-start.2 = (bf16[1,128,1024]{2,1,0:T(8,128)(2,1)}, bf16[1,128,1024]{2,1,0:T(8,128)(2,1)S(1)}, u32[]{:S(2)}, u32[]{:S(2)}) collective-permute-start(bf16[1,128,1024]{2,1,0:T(8,128)(2,1)} %get-tuple-element.24), channel_id=1, source_target_pairs={{0,3},{1,2},{2,1},{3,0},{4,7},{5,6},{6,5},{7,4},{8,11},{9,10},{10,... | collective-permute-start | bytes 786440 | tf_op jit(solution)/shard_map/ppermute | solution.py:221
  151.4 20.5 %all-to-all-start.4 = ((bf16[4,128,256]{2,1,0:T(8,128)(2,1)}), bf16[4,128,256]{2,1,0:T(8,128)(2,1)S(1)}, u32[]{:S(2)}, u32[]{:S(2)}) async-start(bf16[4,128,256]{2,1,0:T(8,128)(2,1)} %bitcast.10), calls=%async_computation.4 | async-start | bytes 524288 | tf_op jit(solution)/shard_map/all_to_all | solution.py:173
Sparse Core Ops, SparseCore 0:
  19.4 49.9 all-gather.1

commit v4 on v3

--- a/solution.py
+++ b/solution.py
@@ -156,6 +156,97 @@
     )(places, starts, inverse, qd, delta, kv)
 
 
+def gather_kernel(parts, team, k_ref, v_ref, out_ref, near_send, near_recv, far_send, far_recv):
+    me = lax.axis_index("ctx")
+    other = lax.axis_index("head")
+    mine = me % team
+    block = me // team
+    half = parts // 2
+    side = block % 2
+    turn = (1 - side) * (block // 2) + side * (parts - 1 - block // 2)
+    rows = k_ref.shape[0]
+
+    def block_of(place):
+        place = (place + parts) % parts
+        upper = place // half
+        return (1 - upper) * 2 * place + upper * (2 * (parts - 1 - place) + 1)
+
+    right = block_of(turn + 1) * team + mine
+    left = block_of(turn - 1) * team + mine
+    friends = [block * team + (mine + shift) % team for shift in range(1, team)]
+    barrier = pltpu.get_barrier_semaphore()
+    for device in [left, right] + friends:
+        pl.semaphore_signal(
+            barrier, inc=1, device_id=(device, other), device_id_type=pl.DeviceIdType.MESH
+        )
+    pl.semaphore_wait(barrier, team + 1)
+    home = pl.ds(pl.multiple_of(me * rows, TILE), rows)
+    copies = []
+    for which, ref in enumerate((k_ref, v_ref)):
+        lanes = slice(which * HD, (which + 1) * HD)
+        for shift in range(1, team):
+            source = pl.ds(pl.multiple_of((mine + shift) % team * HD, HD), HD)
+            copy = pltpu.make_async_remote_copy(
+                src_ref=ref.at[:, source],
+                dst_ref=out_ref.at[home, lanes],
+                send_sem=near_send.at[which, shift - 1],
+                recv_sem=near_recv.at[which, shift - 1],
+                device_id=(friends[shift - 1], other),
+                device_id_type=pl.DeviceIdType.MESH,
+            )
+            copy.start()
+            copies.append(copy)
+    for which, ref in enumerate((k_ref, v_ref)):
+        own = pl.ds(pl.multiple_of(mine * HD, HD), HD)
+        out_ref[home, which * HD : (which + 1) * HD] = ref[:, own]
+    for copy in copies:
+        copy.wait_recv()
+    span = team * rows
+    for step in range(half):
+        moves = [(turn - step, right, 0)]
+        if step < half - 1:
+            moves.append((turn + step, left, 1))
+        now = []
+        for place, device, way in moves:
+            area = pl.ds(pl.multiple_of(block_of(place) * span, TILE), span)
+            copy = pltpu.make_async_remote_copy(
+                src_ref=out_ref.at[area],
+                dst_ref=out_ref.at[area],
+                send_sem=far_send.at[way, step],
+                recv_sem=far_recv.at[way, step],
+                device_id=(device, other),
+                device_id_type=pl.DeviceIdType.MESH,
+            )
+            copy.start()
+            now.append(copy)
+            copies.append(copy)
+        for copy in now:
+            copy.wait_recv()
+    for copy in copies:
+        copy.wait_send()
+
+
+def gather_head(key_states, value_states, parts, team):
+    rows = key_states.shape[0]
+    vmem = pl.BlockSpec(memory_space=pltpu.VMEM)
+    return pl.pallas_call(
+        functools.partial(gather_kernel, parts, team),
+        out_shape=jax.ShapeDtypeStruct((parts * team * rows, 2 * HD), jnp.bfloat16),
+        in_specs=[vmem, vmem],
+        out_specs=vmem,
+        scratch_shapes=[
+            pltpu.SemaphoreType.DMA((2, team - 1)),
+            pltpu.SemaphoreType.DMA((2, team - 1)),
+            pltpu.SemaphoreType.DMA((2, parts // 2)),
+            pltpu.SemaphoreType.DMA((2, parts // 2)),
+        ],
+        compiler_params=pltpu.CompilerParams(
+            collective_id=0, has_side_effects=True, vmem_limit_bytes=16 * 1024 * 1024
+        ),
+        cost_estimate=pl.CostEstimate(flops=0, bytes_accessed=100 << 20, transcendentals=0),
+    )(key_states, value_states)
+
+
 def local(queries, key_states, value_states, outputs, out_grad, doc_of_tile, tile_position):
     rows = queries.shape[0]
     kv_heads = key_states.shape[1] // HD
@@ -178,13 +269,10 @@
     products = out_grad.astype(jnp.float32) * outputs.astype(jnp.float32)
     delta = jnp.sum(products.reshape(rows, split * heads, HD), axis=-1)
     if head_count == 1:
-        kv = jnp.concatenate(
-            [key_states.reshape(rows, split, HD), value_states.reshape(rows, split, HD)], axis=2
-        ).reshape(rows, split * 2 * HD)
-        kv = swap(kv, 1, 0)
+        kv_all = gather_head(key_states, value_states, ctx_count // team, team)
     else:
         kv = jnp.concatenate([key_states, value_states], axis=1)
-    kv_all = lax.all_gather(kv, "ctx", axis=0, tiled=True, axis_index_groups=far)
+        kv_all = lax.all_gather(kv, "ctx", axis=0, tiled=True, axis_index_groups=far)
     qd = jnp.concatenate(
         [
             queries.reshape(rows, split, heads * HD),

time: 180 us -> 178 us (0.989)
  Pallas kernels: 28.6 us -> 72.6 us
  waiting for transfers between devices: 80.7 us -> 44.8 us
  between operations: 14.3 us -> 0.87 us
  starting transfers between devices: 15.8 us -> 28.3 us
  blocking collectives: 10.2 us -> 0 us
    pallas_call x0 -> x1, Pallas kernels: none -> 57.6 us  [gather_head(): pl.pallas_call(functools.partial(gather_kernel, parts, team), out_shape=j...]
    all_to_all x3, waiting for transfers between devices: 25.5 us -> 0.89 us  [swap(): lax.all_to_all(value, 'ctx', split_axis, concat_axis, axis_index_groups=n...]
    pallas_call x1, Pallas kernels: 28.6 us -> 15 us  [attention_backward(): pl.pallas_call(functools.partial(kernel, heads, tiles), out_shape=(jax.Sh...]
    all_to_all x1, starting transfers between devices: 3.6 us -> 15.2 us  [local(): dkv = lax.all_to_all(dkv, 'ctx', 0, 0, axis_index_groups=far, tiled=True)]
    all_gather x1 -> x0, waiting for transfers between devices: 10.6 us -> none  [local(): lax.all_gather(kv, 'ctx', axis=0, tiled=True, axis_index_groups=far)]
    all_to_all x1 -> x0, blocking collectives: 10.2 us -> none  [swap(): lax.all_to_all(value, 'ctx', split_axis, concat_axis, axis_index_groups=n...]
    unnamed x14 -> x18, local copies, waits for them, and re-layouts: 5.42 us -> 5.9 us
  transfers between devices with their start and end apart: 8 -> 7, of which waited for: 4 -> 2; matrix products, arithmetic and copies ran while one was open for 14% -> 13% of each run, Pallas kernels for 0% -> 32%
where the time goes in v4:
time: 178 us; the launch traced here: 177 us
  Pallas kernels  72.6 us (41%)
  waiting for transfers between devices  44.8 us (25%)
  starting transfers between devices  28.3 us (16%)
  local copies, waits for them, and re-layouts  25.4 us (14%)
  other arithmetic  5.35 us (3%)
    pallas_call x1, Pallas kernels, gather_head(): pl.pallas_call(functools.partial(gather_kernel, parts, team), out_shape=j...  57.6 us
    all_to_all x1, waiting for transfers between devices, local(): dkv = lax.all_to_all(dkv, 'ctx', 0, 0, axis_index_groups=far, tiled=True)  43.9 us
    all_to_all x1, starting transfers between devices, local(): dkv = lax.all_to_all(dkv, 'ctx', 0, 0, axis_index_groups=far, tiled=True)  15.2 us
    pallas_call x1, Pallas kernels, attention_backward(): pl.pallas_call(functools.partial(kernel, heads, tiles), out_shape=(jax.Sh...  15 us
    dynamic_update_slice x4, local copies, waits for them, and re-layouts, local(): home = lax.dynamic_update_slice_in_dim(home, piece, me ^ shift, 0)  13.7 us
    all_to_all x3, starting transfers between devices, swap(): lax.all_to_all(value, 'ctx', split_axis, concat_axis, axis_index_groups=n...  11.2 us
    unnamed x18, local copies, waits for them, and re-layouts  5.9 us
  transfers between devices with their start and end apart: 7, of which 2 were waited for; matrix products, arithmetic and copies ran while one was open for 13% of the time, Pallas kernels for 32%

profile of v4, /device:TPU:0, one launch (start us, length us, event | category | flops | bytes accessed | tf_op | source)
XLA Modules:
  0.0 177.3 jit_solution(17733605949059575900)
XLA Ops:
  0.6 1.8 %multiply_bitcast_fusion = f32[16,8,32,128]{3,1,2,0:T(8,128)S(1)} fusion(bf16[128,4096]{1,0:T(8,128)(2,1)} %param.10, bf16[128,4096]{1,0:T(8,128)(2,1)} %param.11), kind=kLoop, calls=%fused_computation.2 | loop fusion | flops 1572864 | bytes 4194304
  2.4 0.4 copy.65
  2.8 0.0 copy-start.5
  2.8 0.6 reduce_sum.41
  3.4 0.7 copy.55
  4.1 4.2 %all-to-all-start.1 = ((f32[128,4,8]{0,2,1:T(8,128)}), f32[128,4,8]{0,2,1:T(8,128)S(1)}, u32[]{:S(2)}, u32[]{:S(2)}) async-start(f32[128,4,8]{0,2,1:T(8,128)} %bitcast.2), calls=%async_computation.1 | async-start | bytes 32768 | tf_op jit(solution)/shard_map/all_to_all | solution.py:264
  8.3 0.0 copy-done.5
  8.3 1.4 copy_bitcast_fusion
  9.8 1.5 pad_maximum_fusion
  11.3 0.0 copy-start.6
  11.3 0.0 copy-start.4
  11.3 0.0 copy-start.2
  11.3 0.0 copy-start.3
  11.3 0.9 all-to-all-done.1
  12.2 3.6 %all-to-all-start = ((bf16[128,4,2048]{2,0,1:T(8,128)(2,1)}), bf16[128,4,2048]{2,0,1:T(8,128)(2,1)S(1)}, u32[]{:S(2)}, u32[]{:S(2)}) async-start(bf16[128,4,2048]{2,0,1:T(8,128)(2,1)} %pad_maximum_fusion), calls=%async_computation | async-start | bytes 4194304 | tf_op jit(solution)/shard_map/all_to_all | solution.py:264
  15.8 0.0 copy-done.6
  15.8 0.1 compare_select_fusion
  15.9 0.0 copy-done.4
  15.9 0.6 gather_fusion
  16.6 0.0 copy-done.2
  16.6 0.0 copy-done.3
  16.6 57.6 %shard_map.94.kv_ref = bf16[4096,256]{1,0:T(8,128)(2,1)S(1)} custom-call(bf16[128,512]{1,0:T(8,128)(2,1)S(1)} %copy-done.2, bf16[128,512]{1,0:T(8,128)(2,1)S(1)} %copy-done.3), custom_call_target="tpu_custom_call" | custom-call | bytes 104857600 | tf_op jit(solution)/shard_map/pallas_call | solution.py:232
  74.1 0.0 copy-start
  74.2 1.3 copy-done
  75.5 0.1 select_reduce_fusion.inverse_ref
  75.6 0.2 convert_reduce_fusion.place_start_ref
  75.8 0.0 all-to-all-done
  75.8 15.0 %shard_map.95 = (bf16[512,1024]{1,0:T(8,128)(2,1)S(1)}, bf16[4096,256]{1,0:T(8,128)(2,1)S(1)}) custom-call(s32[4]{0:T(128)S(1)} %get-tuple-element.23.place_ref, s32[4]{0:T(128)S(1)} %convert_reduce_fusion.place_start_ref, s32[32]{0:T(128)S(1)} %select_reduce_fusion.inverse_ref, bf16[512,2048]{1,0:T(8,128)(2,1)S(1)} %bitcast.26, f32[4,1,1024]{2,1,0:T(1,128)S(1)} %bitcast.29, ...), custom_call_target="tpu_custom_call" | custom-call | flops 6442450944 | bytes 12582912 | tf_op jit(solution)/shard_map/pallas_call | solution.py:135
  90.8 0.0 copy-start.1
  90.8 1.3 copy-done.1
  92.1 15.2 %all-to-all-start.2 = ((bf16[8,512,256]{2,1,0:T(8,128)(2,1)}), bf16[8,512,256]{2,1,0:T(8,128)(2,1)S(1)}, u32[]{:S(2)}, u32[]{:S(2)}) async-start(bf16[8,512,256]{2,1,0:T(8,128)(2,1)} %bitcast.27), calls=%async_computation.2 | async-start | bytes 4194304 | tf_op jit(solution)/shard_map/all_to_all | solution.py:312
  107.4 0.9 constant_dynamic-slice_fusion
  108.3 0.0 collective-permute-start
  108.3 0.7 collective-permute-start.1
  109.0 1.2 collective-permute-start.2
  110.1 43.9 %all-to-all-done.2 = bf16[8,512,256]{2,1,0:T(8,128)(2,1)S(1)} async-done(((bf16[8,512,256]{2,1,0:T(8,128)(2,1)}), bf16[8,512,256]{2,1,0:T(8,128)(2,1)S(1)}, u32[]{:S(2)}, u32[]{:S(2)}) %all-to-all-start.2) | async-done | bytes 2097184 | tf_op jit(solution)/shard_map/all_to_all | solution.py:312
  154.0 1.0 reduce_sum.42
  155.0 3.4 %all-to-all-start.3 = ((bf16[4,128,256]{2,1,0:T(8,128)(2,1)}), bf16[4,128,256]{2,1,0:T(8,128)(2,1)S(1)}, u32[]{:S(2)}, u32[]{:S(2)}) async-start(bf16[4,128,256]{2,1,0:T(8,128)(2,1)} %bitcast.8), calls=%async_computation.3 | async-start | bytes 524288 | tf_op jit(solution)/shard_map/all_to_all | solution.py:264
  158.5 0.4 copy.56
  158.9 0.3 broadcast_in_dim.23
  159.2 3.4 %dynamic_update_slice.12 = bf16[4,128,1024]{2,0,1:T(4,128)(2,1)S(1)} dynamic-update-slice(bf16[4,128,1024]{2,0,1:T(4,128)(2,1)S(1)} %broadcast_in_dim.23, bf16[1,128,1024]{2,0,1:T(2,128)(2,1)S(1)} %copy.56, s32[]{:T(128)S(6)} %select_n.36, s32[]{:T(128)} %constant.37.clone.1, s32[]{:T(128)} %constant.37.clone.1) | dynamic-update-slice | bytes 524292 | tf_op jit(solution)/shard_map/dynamic_update_slice | solution.py:310
  162.6 0.0 collective-permute-done
  162.6 0.4 copy.57
  163.0 3.4 %dynamic_update_slice.13 = bf16[4,128,1024]{2,0,1:T(4,128)(2,1)S(1)} dynamic-update-slice(bf16[4,128,1024]{2,0,1:T(4,128)(2,1)S(1)} %dynamic_update_slice.12, bf16[1,128,1024]{2,0,1:T(2,128)(2,1)S(1)} %copy.57, s32[]{:T(128)S(6)} %select_n.37, s32[]{:T(128)} %constant.37.clone.1, s32[]{:T(128)} %constant.37.clone.1) | dynamic-update-slice | bytes 524292 | tf_op jit(solution)/shard_map/dynamic_update_slice | solution.py:310
  166.5 0.0 collective-permute-done.1
  166.5 0.4 copy.58
  166.9 3.4 %dynamic_update_slice.14 = bf16[4,128,1024]{2,0,1:T(4,128)(2,1)S(1)} dynamic-update-slice(bf16[4,128,1024]{2,0,1:T(4,128)(2,1)S(1)} %dynamic_update_slice.13, bf16[1,128,1024]{2,0,1:T(2,128)(2,1)S(1)} %copy.58, s32[]{:T(128)S(6)} %select_n.38, s32[]{:T(128)} %constant.37.clone.1, s32[]{:T(128)} %constant.37.clone.1) | dynamic-update-slice | bytes 524292 | tf_op jit(solution)/shard_map/dynamic_update_slice | solution.py:310
  170.3 0.0 collective-permute-done.2
  170.3 0.4 copy.59
  170.8 3.4 %dynamic_update_slice.15 = bf16[4,128,1024]{2,0,1:T(4,128)(2,1)S(1)} dynamic-update-slice(bf16[4,128,1024]{2,0,1:T(4,128)(2,1)S(1)} %dynamic_update_slice.14, bf16[1,128,1024]{2,0,1:T(2,128)(2,1)S(1)} %copy.59, s32[]{:T(128)S(6)} %select_n.39, s32[]{:T(128)} %constant.37.clone.1, s32[]{:T(128)} %constant.37.clone.1) | dynamic-update-slice | bytes 524292 | tf_op jit(solution)/shard_map/dynamic_update_slice | solution.py:310
  174.2 1.3 copy.66
  175.5 0.0 all-to-all-done.3
  175.5 0.2 copy.60
  175.7 0.8 copy.61
  176.5 0.8 copy.62
  (2 shorter events, 0.0 us)
Async XLA Ops:
  2.8 5.5 %copy-start.5 = (bf16[128,4096]{1,0:T(8,128)(2,1)S(1)}, bf16[128,4096]{1,0:T(8,128)(2,1)}, u32[]{:S(2)}) copy-start(bf16[128,4096]{1,0:T(8,128)(2,1)} %param.11) | copy-start | bytes 3145732
  4.1 8.1 %all-to-all-start.1 = ((f32[128,4,8]{0,2,1:T(8,128)}), f32[128,4,8]{0,2,1:T(8,128)S(1)}, u32[]{:S(2)}, u32[]{:S(2)}) async-start(f32[128,4,8]{0,2,1:T(8,128)} %bitcast.2), calls=%async_computation.1 | async-start | bytes 32768 | tf_op jit(solution)/shard_map/all_to_all | solution.py:264
  11.3 4.5 %copy-start.6 = (s32[32]{0:T(128)S(1)}, s32[32]{0:T(128)}, u32[]{:S(2)}) copy-start(s32[32]{0:T(128)} %param.13) | copy-start | bytes 388
  11.3 4.6 %copy-start.4 = (s32[32]{0:T(128)S(1)}, s32[32]{0:T(128)}, u32[]{:S(2)}) copy-start(s32[32]{0:T(128)} %param.12) | copy-start | bytes 388
  11.3 5.3 %copy-start.2 = (bf16[128,512]{1,0:T(8,128)(2,1)S(1)}, bf16[128,512]{1,0:T(8,128)(2,1)}, u32[]{:S(2)}) copy-start(bf16[128,512]{1,0:T(8,128)(2,1)} %k_ref.1) | copy-start | bytes 393220
  11.3 5.3 %copy-start.3 = (bf16[128,512]{1,0:T(8,128)(2,1)S(1)}, bf16[128,512]{1,0:T(8,128)(2,1)}, u32[]{:S(2)}) copy-start(bf16[128,512]{1,0:T(8,128)(2,1)} %v_ref.1) | copy-start | bytes 393220
  12.2 63.6 %all-to-all-start = ((bf16[128,4,2048]{2,0,1:T(8,128)(2,1)}), bf16[128,4,2048]{2,0,1:T(8,128)(2,1)S(1)}, u32[]{:S(2)}, u32[]{:S(2)}) async-start(bf16[128,4,2048]{2,0,1:T(8,128)(2,1)} %pad_maximum_fusion), calls=%async_computation | async-start | bytes 4194304 | tf_op jit(solution)/shard_map/all_to_all | solution.py:264
  74.1 1.3 copy-start
  90.8 1.3 copy-start.1
  92.1 61.9 %all-to-all-start.2 = ((bf16[8,512,256]{2,1,0:T(8,128)(2,1)}), bf16[8,512,256]{2,1,0:T(8,128)(2,1)S(1)}, u32[]{:S(2)}, u32[]{:S(2)}) async-start(bf16[8,512,256]{2,1,0:T(8,128)(2,1)} %bitcast.27), calls=%async_computation.2 | async-start | bytes 4194304 | tf_op jit(solution)/shard_map/all_to_all | solution.py:312
  108.3 54.3 %collective-permute-start = (bf16[1,128,1024]{2,1,0:T(8,128)(2,1)}, bf16[1,128,1024]{2,1,0:T(8,128)(2,1)S(1)}, u32[]{:S(2)}, u32[]{:S(2)}) collective-permute-start(bf16[1,128,1024]{2,1,0:T(8,128)(2,1)} %get-tuple-element.26), channel_id=1, source_target_pairs={{0,1},{1,0},{2,3},{3,2},{4,5},{5,4},{6,7},{7,6},{8,9},{9,8},{10,11... | collective-permute-start | bytes 786440 | tf_op jit(solution)/shard_map/ppermute | solution.py:309
  108.3 58.2 %collective-permute-start.1 = (bf16[1,128,1024]{2,1,0:T(8,128)(2,1)}, bf16[1,128,1024]{2,1,0:T(8,128)(2,1)S(1)}, u32[]{:S(2)}, u32[]{:S(2)}) collective-permute-start(bf16[1,128,1024]{2,1,0:T(8,128)(2,1)} %get-tuple-element.25), channel_id=1, source_target_pairs={{0,2},{1,3},{2,0},{3,1},{4,6},{5,7},{6,4},{7,5},{8,10},{9,11},{10,... | collective-permute-start | bytes 786440 | tf_op jit(solution)/shard_map/ppermute | solution.py:309
  109.0 61.4 %collective-permute-start.2 = (bf16[1,128,1024]{2,1,0:T(8,128)(2,1)}, bf16[1,128,1024]{2,1,0:T(8,128)(2,1)S(1)}, u32[]{:S(2)}, u32[]{:S(2)}) collective-permute-start(bf16[1,128,1024]{2,1,0:T(8,128)(2,1)} %get-tuple-element.24), channel_id=1, source_target_pairs={{0,3},{1,2},{2,1},{3,0},{4,7},{5,6},{6,5},{7,4},{8,11},{9,10},{10,... | collective-permute-start | bytes 786440 | tf_op jit(solution)/shard_map/ppermute | solution.py:309
  155.0 20.5 %all-to-all-start.3 = ((bf16[4,128,256]{2,1,0:T(8,128)(2,1)}), bf16[4,128,256]{2,1,0:T(8,128)(2,1)S(1)}, u32[]{:S(2)}, u32[]{:S(2)}) async-start(bf16[4,128,256]{2,1,0:T(8,128)(2,1)} %bitcast.8), calls=%async_computation.3 | async-start | bytes 524288 | tf_op jit(solution)/shard_map/all_to_all | solution.py:264

commit v5 on v4

--- a/solution.py
+++ b/solution.py
@@ -301,14 +301,20 @@
     if head_count == 1:
         blocks = dq.reshape(team, rows, -1)
         me = ctx_index & (team - 1)
-        home = jnp.zeros_like(blocks)
+        pieces = []
         for shift in range(team):
             piece = lax.dynamic_index_in_dim(blocks, me ^ shift, 0)
             if shift:
                 pairs = [(i, i ^ shift) for i in range(ctx_count)]
                 piece = lax.ppermute(piece, "ctx", pairs)
-            home = lax.dynamic_update_slice_in_dim(home, piece, me ^ shift, 0)
-        dq_home = jnp.transpose(home, (1, 0, 2)).reshape(rows, -1)
+            pieces.append(piece[0])
+        columns = []
+        for head in range(team):
+            chosen = pieces[0]
+            for shift in range(1, team):
+                chosen = jnp.where((me ^ shift) == head, pieces[shift], chosen)
+            columns.append(chosen)
+        dq_home = jnp.concatenate(columns, axis=1)
     dkv = lax.all_to_all(dkv, "ctx", 0, 0, axis_index_groups=far, tiled=True)
     dkv = jnp.sum(dkv.reshape(parts, -1, 2 * HD).astype(jnp.float32), axis=0).astype(jnp.bfloat16)
     if head_count == 1:

time: 178 us -> 166 us (0.933)
  local copies, waits for them, and re-layouts: 25.4 us -> 7.04 us
  starting transfers between devices: 28.3 us -> 33.1 us
  Pallas kernels: 72.6 us -> 69 us
  other arithmetic: 5.35 us -> 8.49 us
  waiting for transfers between devices: 44.8 us -> 47.4 us
    all_to_all x1, waiting for transfers between devices: 43.9 us -> 30 us  [local(): dkv = lax.all_to_all(dkv, 'ctx', 0, 0, axis_index_groups=far, tiled=True)]
    dynamic_update_slice x4 -> x0, local copies, waits for them, and re-layouts: 13.7 us -> none  [local(): home = lax.dynamic_update_slice_in_dim(home, piece, me ^ shift, 0)]
    ppermute x3, waiting for transfers between devices: 0.01 us -> 11.7 us  [local(): piece = lax.ppermute(piece, 'ctx', pairs)]
    all_to_all x3, waiting for transfers between devices: 0.89 us -> 5.81 us  [swap(): lax.all_to_all(value, 'ctx', split_axis, concat_axis, axis_index_groups=n...]
    all_to_all x1, starting transfers between devices: 15.2 us -> 20 us  [local(): dkv = lax.all_to_all(dkv, 'ctx', 0, 0, axis_index_groups=far, tiled=True)]
    pallas_call x1, Pallas kernels: 15 us -> 11.4 us  [attention_backward(): pl.pallas_call(functools.partial(kernel, heads, tiles), out_shape=(jax.Sh...]
    unnamed x18 -> x21, local copies, waits for them, and re-layouts: 5.9 us -> 3.25 us
    select_n x0 -> x1, other arithmetic: none -> 2.09 us  [local(): chosen = jnp.where(me ^ shift == head, pieces[shift], chosen)]
  transfers between devices with their start and end apart: 7 -> 7, of which waited for: 2 -> 5; matrix products, arithmetic and copies ran while one was open for 13% -> 5% of each run, Pallas kernels for 32% -> 35%
where the time goes in v5:
time: 166 us
  Pallas kernels  69 us (42%)
  waiting for transfers between devices  47.4 us (29%)
  starting transfers between devices  33.1 us (20%)
  other arithmetic  8.49 us (5%)
  local copies, waits for them, and re-layouts  7.04 us (4%)
    pallas_call x1, Pallas kernels, gather_head(): pl.pallas_call(functools.partial(gather_kernel, parts, team), out_shape=j...  57.6 us
    all_to_all x1, waiting for transfers between devices, local(): dkv = lax.all_to_all(dkv, 'ctx', 0, 0, axis_index_groups=far, tiled=True)  30 us
    all_to_all x1, starting transfers between devices, local(): dkv = lax.all_to_all(dkv, 'ctx', 0, 0, axis_index_groups=far, tiled=True)  20 us
    ppermute x3, waiting for transfers between devices, local(): piece = lax.ppermute(piece, 'ctx', pairs)  11.7 us
    pallas_call x1, Pallas kernels, attention_backward(): pl.pallas_call(functools.partial(kernel, heads, tiles), out_shape=(jax.Sh...  11.4 us
    all_to_all x3, starting transfers between devices, swap(): lax.all_to_all(value, 'ctx', split_axis, concat_axis, axis_index_groups=n...  11.2 us
    all_to_all x3, waiting for transfers between devices, swap(): lax.all_to_all(value, 'ctx', split_axis, concat_axis, axis_index_groups=n...  5.81 us
  transfers between devices with their start and end apart: 7, of which 5 were waited for; matrix products, arithmetic and copies ran while one was open for 5% of the time, Pallas kernels for 35%

profile of v5, /device:TPU:0, one launch (start us, length us, event | category | flops | bytes accessed | tf_op | source)
XLA Modules:
  0.0 165.9 jit_solution(14659023076860044911)
XLA Ops:
  0.6 1.8 %multiply_bitcast_fusion = f32[16,8,32,128]{3,1,2,0:T(8,128)S(1)} fusion(bf16[128,4096]{1,0:T(8,128)(2,1)} %param.10, bf16[128,4096]{1,0:T(8,128)(2,1)} %param.11), kind=kLoop, calls=%fused_computation.2 | loop fusion | flops 1572864 | bytes 4194304
  2.4 0.4 copy.41
  2.8 0.0 copy-start.4
  2.8 0.6 reduce_sum.41
  3.4 0.7 copy.35
  4.1 4.2 %all-to-all-start.1 = ((f32[128,4,8]{0,2,1:T(8,128)}), f32[128,4,8]{0,2,1:T(8,128)S(1)}, u32[]{:S(2)}, u32[]{:S(2)}) async-start(f32[128,4,8]{0,2,1:T(8,128)} %bitcast.2), calls=%async_computation.1 | async-start | bytes 32768 | tf_op jit(solution)/shard_map/all_to_all | solution.py:264
  8.3 0.0 copy-done.4
  8.3 1.4 copy_bitcast_fusion
  9.8 1.5 pad_maximum_fusion
  11.3 0.0 copy-start.8
  11.3 0.0 copy-start.3
  11.3 0.0 copy-start.1
  11.3 0.0 copy-start.2
  11.3 0.9 all-to-all-done.1
  12.2 3.6 %all-to-all-start = ((bf16[128,4,2048]{2,0,1:T(8,128)(2,1)}), bf16[128,4,2048]{2,0,1:T(8,128)(2,1)S(1)}, u32[]{:S(2)}, u32[]{:S(2)}) async-start(bf16[128,4,2048]{2,0,1:T(8,128)(2,1)} %pad_maximum_fusion), calls=%async_computation | async-start | bytes 4194304 | tf_op jit(solution)/shard_map/all_to_all | solution.py:264
  15.8 0.0 copy-done.8
  15.8 0.1 compare_select_fusion
  15.9 0.0 copy-done.3
  15.9 0.6 gather_fusion
  16.6 0.0 copy-done.1
  16.6 0.0 copy-done.2
  16.6 57.6 %shard_map.94.kv_ref = bf16[4096,256]{1,0:T(8,128)(2,1)S(1)} custom-call(bf16[128,512]{1,0:T(8,128)(2,1)S(1)} %copy-done.1, bf16[128,512]{1,0:T(8,128)(2,1)S(1)} %copy-done.2), custom_call_target="tpu_custom_call" | custom-call | bytes 104857600 | tf_op jit(solution)/shard_map/pallas_call | solution.py:232
  74.1 0.0 copy-start
  74.2 1.3 copy-done
  75.5 0.1 select_reduce_fusion.inverse_ref
  75.6 0.2 convert_reduce_fusion.place_start_ref
  75.8 0.0 all-to-all-done
  75.8 11.4 %shard_map.95 = (bf16[512,1024]{1,0:T(8,128)(2,1)S(1)}, bf16[4096,256]{1,0:T(8,128)(2,1)}) custom-call(s32[4]{0:T(128)S(1)} %get-tuple-element.23.place_ref, s32[4]{0:T(128)S(1)} %convert_reduce_fusion.place_start_ref, s32[32]{0:T(128)S(1)} %select_reduce_fusion.inverse_ref, bf16[512,2048]{1,0:T(8,128)(2,1)S(1)} %bitcast.31, f32[4,1,1024]{2,1,0:T(1,128)S(1)} %bitcast.34, ...), custom_call_target="tpu_custom_call" | custom-call | flops 6442450944 | bytes 12582912 | tf_op jit(solution)/shard_map/pallas_call | solution.py:135
  87.2 20.0 %all-to-all-start.2 = ((bf16[8,512,256]{2,1,0:T(8,128)(2,1)}), bf16[8,512,256]{2,1,0:T(8,128)(2,1)S(1)}, u32[]{:S(2)}, u32[]{:S(2)}) async-start(bf16[8,512,256]{2,1,0:T(8,128)(2,1)} %bitcast.10), calls=%async_computation.2 | async-start | bytes 4194304 | tf_op jit(solution)/shard_map/all_to_all | solution.py:318
  107.3 0.8 constant_dynamic-slice_fusion
  108.1 0.0 collective-permute-start
  108.1 0.9 collective-permute-start.1
  109.0 0.9 collective-permute-start.2
  110.0 7.0 %collective-permute-done = bf16[1,128,1024]{2,1,0:T(8,128)(2,1)} collective-permute-done((bf16[1,128,1024]{2,1,0:T(8,128)(2,1)}, bf16[1,128,1024]{2,1,0:T(8,128)(2,1)}, u32[]{:S(2)}, u32[]{:S(2)}) %collective-permute-start) | collective-permute-done | bytes 262176 | tf_op jit(solution)/shard_map/ppermute | solution.py:309
  117.0 4.7 %collective-permute-done.1 = bf16[1,128,1024]{2,1,0:T(8,128)(2,1)} collective-permute-done((bf16[1,128,1024]{2,1,0:T(8,128)(2,1)}, bf16[1,128,1024]{2,1,0:T(8,128)(2,1)}, u32[]{:S(2)}, u32[]{:S(2)}) %collective-permute-start.1) | collective-permute-done | bytes 262176 | tf_op jit(solution)/shard_map/ppermute | solution.py:309
  121.6 0.0 collective-permute-done.2
  121.6 2.1 %select_bitcast_fusion.3 = (bf16[128,1024]{1,0:T(8,128)(2,1)S(1)}, bf16[128,1024]{1,0:T(8,128)(2,1)}, bf16[128,1024]{1,0:T(8,128)(2,1)}, bf16[128,1024]{1,0:T(8,128)(2,1)}) fusion(bf16[1,128,1024]{2,1,0:T(8,128)(2,1)} %collective-permute-done, bf16[1,128,1024]{2,1,0:T(8,128)(2,1)} %collective-permute-done.1, bf16[1,128,1024]{2,1,0:T(8,128)(2,1)} %collective-permute-done.2, ...), kind=kLoop, calls=%fused_computation.9 | loop fusion | flops 1572864 | bytes 2097168 | tf_op jit(solution)/shard_map/jit(_where)/select_n | solution.py:315
  123.7 0.0 copy-start.5
  123.7 0.0 copy-start.6
  123.7 0.0 copy-start.7
  123.7 30.0 %all-to-all-done.2 = bf16[8,512,256]{2,1,0:T(8,128)(2,1)S(1)} async-done(((bf16[8,512,256]{2,1,0:T(8,128)(2,1)}), bf16[8,512,256]{2,1,0:T(8,128)(2,1)S(1)}, u32[]{:S(2)}, u32[]{:S(2)}) %all-to-all-start.2) | async-done | bytes 2097184 | tf_op jit(solution)/shard_map/all_to_all | solution.py:318
  153.7 1.0 reduce_sum.42
  154.7 3.4 %all-to-all-start.3 = ((bf16[4,128,256]{2,1,0:T(8,128)(2,1)}), bf16[4,128,256]{2,1,0:T(8,128)(2,1)S(1)}, u32[]{:S(2)}, u32[]{:S(2)}) async-start(bf16[4,128,256]{2,1,0:T(8,128)(2,1)} %bitcast.11), calls=%async_computation.3 | async-start | bytes 524288 | tf_op jit(solution)/shard_map/all_to_all | solution.py:264
  158.1 0.0 copy-done.5
  158.2 0.0 copy-done.6
  158.2 0.0 copy-done.7
  158.2 1.0 pad_maximum_fusion.1
  159.2 4.9 %all-to-all-done.3 = bf16[4,128,256]{2,1,0:T(8,128)(2,1)S(1)} async-done(((bf16[4,128,256]{2,1,0:T(8,128)(2,1)}), bf16[4,128,256]{2,1,0:T(8,128)(2,1)S(1)}, u32[]{:S(2)}, u32[]{:S(2)}) %all-to-all-start.3) | async-done | bytes 262176 | tf_op jit(solution)/shard_map/all_to_all | solution.py:264
  164.2 0.2 copy.36
  164.4 0.8 copy.37
  165.1 0.8 copy.38
  (2 shorter events, 0.0 us)
Async XLA Ops:
  2.8 5.5 %copy-start.4 = (bf16[128,4096]{1,0:T(8,128)(2,1)S(1)}, bf16[128,4096]{1,0:T(8,128)(2,1)}, u32[]{:S(2)}) copy-start(bf16[128,4096]{1,0:T(8,128)(2,1)} %param.11) | copy-start | bytes 3145732
  4.1 8.1 %all-to-all-start.1 = ((f32[128,4,8]{0,2,1:T(8,128)}), f32[128,4,8]{0,2,1:T(8,128)S(1)}, u32[]{:S(2)}, u32[]{:S(2)}) async-start(f32[128,4,8]{0,2,1:T(8,128)} %bitcast.2), calls=%async_computation.1 | async-start | bytes 32768 | tf_op jit(solution)/shard_map/all_to_all | solution.py:264
  11.3 4.5 %copy-start.8 = (s32[32]{0:T(128)S(1)}, s32[32]{0:T(128)}, u32[]{:S(2)}) copy-start(s32[32]{0:T(128)} %param.13) | copy-start | bytes 388
  11.3 4.6 %copy-start.3 = (s32[32]{0:T(128)S(1)}, s32[32]{0:T(128)}, u32[]{:S(2)}) copy-start(s32[32]{0:T(128)} %param.12) | copy-start | bytes 388
  11.3 5.3 %copy-start.1 = (bf16[128,512]{1,0:T(8,128)(2,1)S(1)}, bf16[128,512]{1,0:T(8,128)(2,1)}, u32[]{:S(2)}) copy-start(bf16[128,512]{1,0:T(8,128)(2,1)} %k_ref.1) | copy-start | bytes 393220
  11.3 5.3 %copy-start.2 = (bf16[128,512]{1,0:T(8,128)(2,1)S(1)}, bf16[128,512]{1,0:T(8,128)(2,1)}, u32[]{:S(2)}) copy-start(bf16[128,512]{1,0:T(8,128)(2,1)} %v_ref.1) | copy-start | bytes 393220
  12.2 63.6 %all-to-all-start = ((bf16[128,4,2048]{2,0,1:T(8,128)(2,1)}), bf16[128,4,2048]{2,0,1:T(8,128)(2,1)S(1)}, u32[]{:S(2)}, u32[]{:S(2)}) async-start(bf16[128,4,2048]{2,0,1:T(8,128)(2,1)} %pad_maximum_fusion), calls=%async_computation | async-start | bytes 4194304 | tf_op jit(solution)/shard_map/all_to_all | solution.py:264
  74.1 1.3 copy-start
  87.2 66.5 %all-to-all-start.2 = ((bf16[8,512,256]{2,1,0:T(8,128)(2,1)}), bf16[8,512,256]{2,1,0:T(8,128)(2,1)S(1)}, u32[]{:S(2)}, u32[]{:S(2)}) async-start(bf16[8,512,256]{2,1,0:T(8,128)(2,1)} %bitcast.10), calls=%async_computation.2 | async-start | bytes 4194304 | tf_op jit(solution)/shard_map/all_to_all | solution.py:318
  108.1 8.9 %collective-permute-start = (bf16[1,128,1024]{2,1,0:T(8,128)(2,1)}, bf16[1,128,1024]{2,1,0:T(8,128)(2,1)}, u32[]{:S(2)}, u32[]{:S(2)}) collective-permute-start(bf16[1,128,1024]{2,1,0:T(8,128)(2,1)} %get-tuple-element.30), channel_id=1, source_target_pairs={{0,3},{1,2},{2,1},{3,0},{4,7},{5,6},{6,5},{7,4},{8,11},{9,10},{10,... | collective-permute-start | bytes 786440 | tf_op jit(solution)/shard_map/ppermute | solution.py:309
  108.1 13.5 %collective-permute-start.1 = (bf16[1,128,1024]{2,1,0:T(8,128)(2,1)}, bf16[1,128,1024]{2,1,0:T(8,128)(2,1)}, u32[]{:S(2)}, u32[]{:S(2)}) collective-permute-start(bf16[1,128,1024]{2,1,0:T(8,128)(2,1)} %get-tuple-element.29), channel_id=1, source_target_pairs={{0,2},{1,3},{2,0},{3,1},{4,6},{5,7},{6,4},{7,5},{8,10},{9,11},{10,... | collective-permute-start | bytes 786440 | tf_op jit(solution)/shard_map/ppermute | solution.py:309
  109.0 12.6 %collective-permute-start.2 = (bf16[1,128,1024]{2,1,0:T(8,128)(2,1)S(1)}, bf16[1,128,1024]{2,1,0:T(8,128)(2,1)}, u32[]{:S(2)}, u32[]{:S(2)}) collective-permute-start(bf16[1,128,1024]{2,1,0:T(8,128)(2,1)S(1)} %get-tuple-element.28), channel_id=1, source_target_pairs={{0,1},{1,0},{2,3},{3,2},{4,5},{5,4},{6,7},{7,6},{8,9},{9,8},{10,11... | collective-permute-start | bytes 786440 | tf_op jit(solution)/shard_map/ppermute | solution.py:309
  123.7 34.4 %copy-start.5 = (bf16[128,1024]{1,0:T(8,128)(2,1)S(1)}, bf16[128,1024]{1,0:T(8,128)(2,1)}, u32[]{:S(2)}) copy-start(bf16[128,1024]{1,0:T(8,128)(2,1)} %get-tuple-element.25) | copy-start | bytes 786436
  123.7 34.4 %copy-start.6 = (bf16[128,1024]{1,0:T(8,128)(2,1)S(1)}, bf16[128,1024]{1,0:T(8,128)(2,1)}, u32[]{:S(2)}) copy-start(bf16[128,1024]{1,0:T(8,128)(2,1)} %get-tuple-element.26) | copy-start | bytes 786436
  123.7 34.4 %copy-start.7 = (bf16[128,1024]{1,0:T(8,128)(2,1)S(1)}, bf16[128,1024]{1,0:T(8,128)(2,1)}, u32[]{:S(2)}) copy-start(bf16[128,1024]{1,0:T(8,128)(2,1)} %get-tuple-element.27) | copy-start | bytes 786436
  154.7 9.4 %all-to-all-start.3 = ((bf16[4,128,256]{2,1,0:T(8,128)(2,1)}), bf16[4,128,256]{2,1,0:T(8,128)(2,1)S(1)}, u32[]{:S(2)}, u32[]{:S(2)}) async-start(bf16[4,128,256]{2,1,0:T(8,128)(2,1)} %bitcast.11), calls=%async_computation.3 | async-start | bytes 524288 | tf_op jit(solution)/shard_map/all_to_all | solution.py:264
